TPU v7x, 128 devices: a whole 4x4x4 slice. The times are simulated.
128 devices in a mesh: ctx: 32 (over x, z, core), wsh: 4 (over y).
Axes of the slice: x: 4, y: 4, z: 4, core: 2. Of those that a mesh axis runs over, the one named last changes fastest.
Arguments:
- tokens: bfloat16 [4, 4096, 768], P('wsh', 'ctx'), may hold values from -6 to 6
- cotangent: bfloat16 [4, 4096, 768], P('wsh', 'ctx'), may hold values from -6 to 6
- pair_of_device: int32 [32], replicated, may hold values from 0 to 31, each once
- qkv_weight: float32 [1, 768, 2304], P(None, ('ctx', 'wsh')), may hold values from -0.3125 to 0.3125
- out_weight: float32 [1, 768, 768], P(None, ('ctx', 'wsh')), may hold values from -1 to 1
- fc1_weight: float32 [1, 768, 3072], P(None, ('ctx', 'wsh')), may hold values from -0.21875 to 0.21875
- fc2_weight: float32 [1, 768, 3072], P(None, ('ctx', 'wsh')), may hold values from -0.109375 to 0.109375
- vectors: float32 [1, 12, 768], replicated, may hold values from -2.5 to 2.5, as said below
- qkv_moment: float32 [1, 768, 2304], P(None, ('ctx', 'wsh')), may hold values from -80 to 80
- qkv_second: float32 [1, 768, 2304], P(None, ('ctx', 'wsh')), may hold values from 8.192 to 131.072
- out_moment: float32 [1, 768, 768], P(None, ('ctx', 'wsh')), may hold values from -32 to 32
- out_second: float32 [1, 768, 768], P(None, ('ctx', 'wsh')), may hold values from 1.31072 to 21.2992
- fc1_moment: float32 [1, 768, 3072], P(None, ('ctx', 'wsh')), may hold values from -40 to 40
- fc1_second: float32 [1, 768, 3072], P(None, ('ctx', 'wsh')), may hold values from 2.048 to 32.768
- fc2_moment: float32 [1, 768, 3072], P(None, ('ctx', 'wsh')), may hold values from -80 to 80
- fc2_second: float32 [1, 768, 3072], P(None, ('ctx', 'wsh')), may hold values from 6.5536 to 106.496
- vector_moment: float32 [1, 12, 768], replicated, may hold values from -80 to 80
- vector_second: float32 [1, 12, 768], replicated, may hold values from 8.192 to 131.072
Outputs:
- block_out: float32 [4, 4096, 768], P('wsh', 'ctx')
- input_grad: float32 [4, 4096, 768], P('wsh', 'ctx')
- qkv_moment_new: float32 [1, 768, 2304], P(None, ('ctx', 'wsh'))
- qkv_second_new: float32 [1, 768, 2304], P(None, ('ctx', 'wsh'))
- qkv_weight_new: float32 [1, 768, 2304], P(None, ('ctx', 'wsh'))
- out_moment_new: float32 [1, 768, 768], P(None, ('ctx', 'wsh'))
- out_second_new: float32 [1, 768, 768], P(None, ('ctx', 'wsh'))
- out_weight_new: float32 [1, 768, 768], P(None, ('ctx', 'wsh'))
- fc1_moment_new: float32 [1, 768, 3072], P(None, ('ctx', 'wsh'))
- fc1_second_new: float32 [1, 768, 3072], P(None, ('ctx', 'wsh'))
- fc1_weight_new: float32 [1, 768, 3072], P(None, ('ctx', 'wsh'))
- fc2_moment_new: float32 [1, 768, 3072], P(None, ('ctx', 'wsh'))
- fc2_second_new: float32 [1, 768, 3072], P(None, ('ctx', 'wsh'))
- fc2_weight_new: float32 [1, 768, 3072], P(None, ('ctx', 'wsh'))
- vector_moment_new: float32 [1, 12, 768], replicated
- vector_second_new: float32 [1, 12, 768], replicated
- vector_new: float32 [1, 12, 768], replicated
Inputs may be any that keep to these rules, and one draw needn't show every extreme that they name: `pair_of_device`: each pair number appears once. `vectors`: rows 0 and 5 of each layer are positive.
All inputs are finite; a program needn't handle non-finite values.
Results may differ from a plain program's by a relative error of at most 0.017.
The roundings to bfloat16 on the way count: a program that leaves them out, or rounds other values in their place, can miss the bound.
Values may be sent and summed in bfloat16 or wider, within the bound.
No kernel may reach another device: no remote copies, remote signals or barrier semaphores. Data moves between devices by JAX's collectives and lax.ppermute only.
A program may use at most 192 MiB of HBM per device.

v0:
```python
import jax
import jax.numpy as jnp
from jax import lax
from jax.sharding import PartitionSpec as P

D = 768
HEADS = 12
HD = 64
FF = 3072
LAYERS = 1
STEP = 5


EPS_NORM = 1e-05
NEGATIVE = -1e30
BETA_ONE = 0.9
BETA_TWO = 0.999
RATE_MATRIX = 0.1
RATE_VECTOR = 0.5
DECAY_MATRIX = 0.1
EPS_ADAM = 1e-08


def layer_norm(hidden, norm_gain, norm_shift):
    center = hidden - jnp.mean(hidden, axis=-1, keepdims=True)
    spread = jnp.mean(center * center, axis=-1, keepdims=True)
    return center * lax.rsqrt(spread + EPS_NORM) * norm_gain + norm_shift


def place_rows(pair_of_device, start_row, row_span, shard_rows):
    row_index = start_row + jnp.arange(row_span, dtype=jnp.int32)
    device = row_index // shard_rows
    within = row_index % shard_rows
    half_rows = shard_rows // 2
    devices = pair_of_device.shape[0]
    matched = device[:, None] == jnp.arange(devices, dtype=jnp.int32)[None, :]
    pair_num = jnp.sum(jnp.where(matched, pair_of_device[None, :], 0), axis=1)
    block_num = jnp.where(within < half_rows, pair_num, 2 * devices - 1 - pair_num)
    return block_num * half_rows + within % half_rows


def block_rows(total_rows, shard_rows):
    shards = total_rows // shard_rows
    per_block = max(1, min(shards, 512 // shard_rows))
    while shards % per_block:
        per_block = per_block - 1
    return per_block * shard_rows


def split_blocks(source, step_rows):
    return source.reshape((source.shape[0] // step_rows, step_rows) + source.shape[1:])


def head_scores(query_part, key_part, query_places, key_places):
    scores = jnp.einsum(
        "qhd,khd->hqk", query_part, key_part, preferred_element_type=jnp.float32
    ) * HD ** (-0.5)
    allowed = key_places[None, None, :] <= query_places[None, :, None]
    return (scores, allowed)


def weight_term(parts):
    normed, back_mixed, attended, branch_low, normed_two, up_low, down_low, active = parts
    return jnp.concatenate(
        [
            jnp.einsum("rc,re->ce", normed, back_mixed, preferred_element_type=jnp.float32),
            jnp.einsum("rc,re->ce", attended, branch_low, preferred_element_type=jnp.float32),
            jnp.einsum("rc,re->ce", normed_two, up_low, preferred_element_type=jnp.float32),
            jnp.einsum("rc,re->ce", down_low, active, preferred_element_type=jnp.float32),
        ],
        axis=1,
    )


def sum_rows(term_fn, shard_width):
    return lax.psum_scatter(
        term_fn(jnp.int32(0), shard_width * lax.axis_size(("ctx", "wsh"))),
        ("ctx", "wsh"),
        scatter_dimension=0,
        tiled=True,
    )


def adamw(weight, moment, second, gradient, step_rate, decay_rate):
    moment_new = BETA_ONE * moment + (1.0 - BETA_ONE) * gradient
    second_new = BETA_TWO * second + (1.0 - BETA_TWO) * gradient * gradient
    moment_hat = moment_new / (1.0 - BETA_ONE**STEP)
    second_hat = second_new / (1.0 - BETA_TWO**STEP)
    weight_new = weight - step_rate * (
        moment_hat / (jnp.sqrt(second_hat) + EPS_ADAM) + decay_rate * weight
    )
    return (moment_new, second_new, weight_new)


def local(
    tokens,
    cotangent,
    pair_of_device,
    qkv_weight,
    out_weight,
    fc1_weight,
    fc2_weight,
    vectors,
    qkv_moment,
    qkv_second,
    out_moment,
    out_second,
    fc1_moment,
    fc1_second,
    fc2_moment,
    fc2_second,
    vector_moment,
    vector_second,
):
    shard_rows = tokens.shape[1]
    scale = HD ** (-0.5)
    own_start = lax.axis_index("ctx") * shard_rows
    own_places = place_rows(pair_of_device, own_start, shard_rows, shard_rows)
    hidden = tokens[0].astype(jnp.float32)
    layer_at = 0
    vector = vectors[layer_at]
    mix_part = qkv_weight[layer_at].astype(jnp.bfloat16)
    proj_part = out_weight[layer_at].astype(jnp.bfloat16)
    up_part = fc1_weight[layer_at].astype(jnp.bfloat16)
    down_part = fc2_weight[layer_at].astype(jnp.bfloat16)
    gathered = (
        lax.all_gather(mix_part, ("ctx", "wsh"), axis=0, tiled=True),
        lax.all_gather(proj_part, ("ctx", "wsh"), axis=0, tiled=True),
        lax.all_gather(up_part, ("ctx", "wsh"), axis=0, tiled=True),
        lax.all_gather(down_part, ("ctx", "wsh"), axis=0, tiled=True),
    )
    gathered_all = [gathered]
    w_mix, w_proj, w_up, w_down = gathered
    normed = layer_norm(hidden, vector[0], vector[1]).astype(jnp.bfloat16)
    projected = jnp.dot(normed, w_mix, preferred_element_type=jnp.float32)
    queries = (projected[:, :D] + vector[2]).astype(jnp.bfloat16)
    key_rows = projected[:, D : 2 * D].astype(jnp.bfloat16)
    value_rows = (projected[:, 2 * D :] + vector[3]).astype(jnp.bfloat16)
    query_heads = queries.reshape(shard_rows, HEADS, HD)
    start_state = (
        jnp.full((HEADS, shard_rows), NEGATIVE, jnp.float32),
        jnp.zeros((HEADS, shard_rows), jnp.float32),
    )
    add_key_piece = lax.all_gather(key_rows, "ctx", axis=0, tiled=True)
    add_piece_rows = add_key_piece.shape[0]
    add_step_rows = block_rows(add_piece_rows, shard_rows)
    add_key_places = place_rows(pair_of_device, jnp.int32(0), add_piece_rows, shard_rows)

    def add_one_step(current, element):
        key_part, place_part = element
        scores, allowed = head_scores(query_heads, key_part, own_places, place_part)
        scores = jnp.where(allowed, scores, NEGATIVE)
        peak_row = jnp.maximum(current[0], jnp.max(scores, axis=-1))
        mass_row = current[1] * jnp.exp(current[0] - peak_row) + jnp.sum(
            jnp.where(allowed, jnp.exp(scores - peak_row[..., None]), 0.0), axis=-1
        )
        return ((peak_row, mass_row), None)

    add_parts = (
        split_blocks(add_key_piece.reshape(add_piece_rows, HEADS, HD), add_step_rows),
        split_blocks(add_key_places, add_step_rows),
    )
    peak_row, mass_row = lax.scan(add_one_step, start_state, add_parts)[0]
    log_total = peak_row + jnp.log(mass_row)

    def add_values(running, pieces, piece_start):
        key_piece, value_piece = pieces
        piece_rows = key_piece.shape[0]
        step_rows = block_rows(piece_rows, shard_rows)
        key_places = place_rows(pair_of_device, piece_start, piece_rows, shard_rows)

        def one_step(current, element):
            key_part, value_part, place_part = element
            scores, allowed = head_scores(query_heads, key_part, own_places, place_part)
            expo = jnp.where(allowed, jnp.exp(scores - log_total[..., None]), 0.0)
            probs = expo.astype(jnp.bfloat16)
            residue = (expo - probs.astype(jnp.float32)).astype(jnp.bfloat16)
            plain = current[0] + jnp.einsum(
                "hqk,khd->qhd", probs, value_part, preferred_element_type=jnp.float32
            )
            extra = current[1] + jnp.einsum(
                "hqk,khd->qhd", residue, value_part, preferred_element_type=jnp.float32
            )
            return ((plain, extra), None)

        parts = (
            split_blocks(key_piece.reshape(piece_rows, HEADS, HD), step_rows),
            split_blocks(value_piece.reshape(piece_rows, HEADS, HD), step_rows),
            split_blocks(key_places, step_rows),
        )
        return lax.scan(one_step, running, parts)[0]

    zero_heads = jnp.zeros((shard_rows, HEADS, HD), jnp.float32)
    plain_sum, extra_sum = add_values(
        (zero_heads, zero_heads),
        (
            lax.all_gather(key_rows, "ctx", axis=0, tiled=True),
            lax.all_gather(value_rows, "ctx", axis=0, tiled=True),
        ),
        jnp.int32(0),
    )
    attended = plain_sum.reshape(shard_rows, D).astype(jnp.bfloat16)
    exact_sum = plain_sum + extra_sum
    branch = jnp.dot(attended, w_proj, preferred_element_type=jnp.float32) + vector[4]
    middle = hidden + branch
    normed_two = layer_norm(middle, vector[5], vector[6]).astype(jnp.bfloat16)
    pre_active = jnp.dot(normed_two, w_up, preferred_element_type=jnp.float32) + vector[
        8:12
    ].reshape(FF)
    active = jax.nn.gelu(pre_active).astype(jnp.bfloat16)
    kept = [
        (
            hidden,
            normed,
            queries,
            key_rows,
            value_rows,
            log_total,
            attended,
            exact_sum,
            middle,
            normed_two,
            pre_active,
            active,
        )
    ]
    hidden = (
        middle
        + jnp.einsum("rf,df->rd", active, w_down, preferred_element_type=jnp.float32)
        + vector[7]
    )
    gradient = cotangent[0].astype(jnp.float32)
    vector_grads = [None] * LAYERS
    weight_rows = [None] * LAYERS
    shard_width = qkv_weight.shape[1]
    for layer_at in reversed(range(LAYERS)):
        (
            hidden_in,
            normed,
            queries,
            key_rows,
            value_rows,
            log_total,
            attended,
            exact_sum,
            middle,
            normed_two,
            pre_active,
            active,
        ) = kept[layer_at]
        vector = vectors[layer_at]
        w_mix, w_proj, w_up, w_down = gathered_all[layer_at]
        down_low = gradient.astype(jnp.bfloat16)
        back_active = jnp.dot(down_low, w_down, preferred_element_type=jnp.float32)
        unused_gelu, gelu_back = jax.vjp(jax.nn.gelu, pre_active)
        up_low = gelu_back(back_active)[0].astype(jnp.bfloat16)
        back_normed_two = jnp.einsum("rf,df->rd", up_low, w_up, preferred_element_type=jnp.float32)
        unused_norm, norm_back = jax.vjp(layer_norm, middle, vector[5], vector[6])
        back_middle, gain_two, shift_two = norm_back(back_normed_two)
        gradient = gradient + back_middle
        branch_low = gradient.astype(jnp.bfloat16)
        back_attended = jnp.einsum(
            "rd,ed->re", branch_low, w_proj, preferred_element_type=jnp.float32
        ).astype(jnp.bfloat16)
        back_heads = back_attended.reshape(shard_rows, HEADS, HD)
        row_dot_rows = jnp.sum(back_heads.astype(jnp.float32) * exact_sum, axis=-1)
        row_dot = row_dot_rows.T
        query_heads = queries.reshape(shard_rows, HEADS, HD)
        own_keys = key_rows.reshape(shard_rows, HEADS, HD)
        own_values = value_rows.reshape(shard_rows, HEADS, HD)

        def add_query_grad(running, pieces, piece_start):
            key_piece, value_piece = pieces
            piece_rows = key_piece.shape[0]
            step_rows = block_rows(piece_rows, shard_rows)
            key_places = place_rows(pair_of_device, piece_start, piece_rows, shard_rows)

            def one_step(current, element):
                key_part, value_part, place_part = element
                scores, allowed = head_scores(query_heads, key_part, own_places, place_part)
                expo = jnp.where(allowed, jnp.exp(scores - log_total[..., None]), 0.0)
                dots = jnp.einsum(
                    "qhd,khd->hqk", back_heads, value_part, preferred_element_type=jnp.float32
                )
                slopes = (expo * (dots - row_dot[..., None])).astype(jnp.bfloat16)
                return (
                    current
                    + jnp.einsum(
                        "hqk,khd->qhd", slopes, key_part, preferred_element_type=jnp.float32
                    ),
                    None,
                )

            parts = (
                split_blocks(key_piece.reshape(piece_rows, HEADS, HD), step_rows),
                split_blocks(value_piece.reshape(piece_rows, HEADS, HD), step_rows),
                split_blocks(key_places, step_rows),
            )
            return lax.scan(one_step, running, parts)[0]

        zero_heads = jnp.zeros((shard_rows, HEADS, HD), jnp.float32)
        query_grad = add_query_grad(
            zero_heads,
            (
                lax.all_gather(key_rows, "ctx", axis=0, tiled=True),
                lax.all_gather(value_rows, "ctx", axis=0, tiled=True),
            ),
            jnp.int32(0),
        )
        all_totals, all_dots = (
            lax.all_gather(log_total.T, "ctx", axis=0, tiled=True),
            lax.all_gather(row_dot_rows, "ctx", axis=0, tiled=True),
        )

        def add_key_grads(running, pieces, piece_start):
            query_piece, back_piece = pieces
            piece_rows = query_piece.shape[0]
            step_rows = block_rows(piece_rows, shard_rows)
            query_places = place_rows(pair_of_device, piece_start, piece_rows, shard_rows)

            def one_step(current, element):
                query_part, back_part, place_part, total_part, dot_part = element
                scores, allowed = head_scores(query_part, own_keys, place_part, own_places)
                expo = jnp.where(allowed, jnp.exp(scores - total_part.T[..., None]), 0.0)
                dots = jnp.einsum(
                    "qhd,khd->hqk", back_part, own_values, preferred_element_type=jnp.float32
                )
                slopes = (expo * (dots - dot_part.T[..., None])).astype(jnp.bfloat16)
                key_grad = current[0] + jnp.einsum(
                    "hqk,qhd->khd", slopes, query_part, preferred_element_type=jnp.float32
                )
                value_grad = current[1] + jnp.einsum(
                    "hqk,qhd->khd",
                    expo.astype(jnp.bfloat16),
                    back_part,
                    preferred_element_type=jnp.float32,
                )
                return ((key_grad, value_grad), None)

            parts = (
                split_blocks(query_piece.reshape(piece_rows, HEADS, HD), step_rows),
                split_blocks(back_piece.reshape(piece_rows, HEADS, HD), step_rows),
                split_blocks(query_places, step_rows),
                split_blocks(all_totals, step_rows),
                split_blocks(all_dots, step_rows),
            )
            return lax.scan(one_step, running, parts)[0]

        key_grad, value_grad = add_key_grads(
            (zero_heads, zero_heads),
            (
                lax.all_gather(queries, "ctx", axis=0, tiled=True),
                lax.all_gather(back_attended, "ctx", axis=0, tiled=True),
            ),
            jnp.int32(0),
        )
        back_queries = (query_grad * scale).reshape(shard_rows, D).astype(jnp.bfloat16)
        back_keys = (key_grad * scale).reshape(shard_rows, D).astype(jnp.bfloat16)
        back_values = value_grad.reshape(shard_rows, D).astype(jnp.bfloat16)
        back_mixed = jnp.concatenate([back_queries, back_keys, back_values], axis=1)
        back_normed = jnp.einsum("re,de->rd", back_mixed, w_mix, preferred_element_type=jnp.float32)
        unused_first, first_back = jax.vjp(layer_norm, hidden_in, vector[0], vector[1])
        back_hidden, gain_one, shift_one = first_back(back_normed)
        gradient = gradient + back_hidden
        up_sums = jnp.sum(up_low.astype(jnp.float32), axis=0).reshape(4, D)
        head_rows = jnp.stack(
            [
                gain_one,
                shift_one,
                jnp.sum(back_queries.astype(jnp.float32), axis=0),
                jnp.sum(back_values.astype(jnp.float32), axis=0),
                jnp.sum(branch_low.astype(jnp.float32), axis=0),
                gain_two,
                shift_two,
                jnp.sum(down_low.astype(jnp.float32), axis=0),
            ],
            axis=0,
        )
        vector_grads[layer_at] = jnp.concatenate([head_rows, up_sums], axis=0)
        layer_parts = (
            normed,
            back_mixed,
            attended,
            branch_low,
            normed_two,
            up_low,
            down_low,
            active,
        )

        def layer_term(start_row, row_span):
            return weight_term(layer_parts)

        weight_rows[layer_at] = sum_rows(layer_term, shard_width)
    stacked = jnp.stack(weight_rows, axis=0)
    vector_total = lax.psum(jnp.stack(vector_grads, axis=0), ("ctx", "wsh"))
    qkv_new = adamw(
        qkv_weight, qkv_moment, qkv_second, stacked[:, :, : 3 * D], RATE_MATRIX, DECAY_MATRIX
    )
    out_new = adamw(
        out_weight, out_moment, out_second, stacked[:, :, 3 * D : 4 * D], RATE_MATRIX, DECAY_MATRIX
    )
    fc1_new = adamw(
        fc1_weight,
        fc1_moment,
        fc1_second,
        stacked[:, :, 4 * D : 4 * D + FF],
        RATE_MATRIX,
        DECAY_MATRIX,
    )
    fc2_new = adamw(
        fc2_weight, fc2_moment, fc2_second, stacked[:, :, 4 * D + FF :], RATE_MATRIX, DECAY_MATRIX
    )
    vec_new = adamw(vectors, vector_moment, vector_second, vector_total, RATE_VECTOR, 0.0)
    return (
        hidden[None],
        gradient[None],
        qkv_new[0],
        qkv_new[1],
        qkv_new[2],
        out_new[0],
        out_new[1],
        out_new[2],
        fc1_new[0],
        fc1_new[1],
        fc1_new[2],
        fc2_new[0],
        fc2_new[1],
        fc2_new[2],
        vec_new[0],
        vec_new[1],
        vec_new[2],
    )


def solution(mesh):
    in_specs = (
        P("wsh", "ctx", None),
        P("wsh", "ctx", None),
        P(),
        P(None, ("ctx", "wsh"), None),
        P(None, ("ctx", "wsh"), None),
        P(None, ("ctx", "wsh"), None),
        P(None, ("ctx", "wsh"), None),
        P(),
        P(None, ("ctx", "wsh"), None),
        P(None, ("ctx", "wsh"), None),
        P(None, ("ctx", "wsh"), None),
        P(None, ("ctx", "wsh"), None),
        P(None, ("ctx", "wsh"), None),
        P(None, ("ctx", "wsh"), None),
        P(None, ("ctx", "wsh"), None),
        P(None, ("ctx", "wsh"), None),
        P(),
        P(),
    )
    out_specs = (
        P("wsh", "ctx", None),
        P("wsh", "ctx", None),
        P(None, ("ctx", "wsh"), None),
        P(None, ("ctx", "wsh"), None),
        P(None, ("ctx", "wsh"), None),
        P(None, ("ctx", "wsh"), None),
        P(None, ("ctx", "wsh"), None),
        P(None, ("ctx", "wsh"), None),
        P(None, ("ctx", "wsh"), None),
        P(None, ("ctx", "wsh"), None),
        P(None, ("ctx", "wsh"), None),
        P(None, ("ctx", "wsh"), None),
        P(None, ("ctx", "wsh"), None),
        P(None, ("ctx", "wsh"), None),
        P(),
        P(),
        P(),
    )
    return jax.shard_map(local, mesh=mesh, in_specs=in_specs, out_specs=out_specs, check_vma=False)
```

profile of v0, /device:TPU:1, one launch (start us, length us, event | category | flops | bytes accessed | tf_op | source)
XLA Modules:
  0.0 1591.5 jit_solution(18403002090633508670)
XLA Ops:
  12.5 71.8 %all-gather.21.cloned.1.call-done = bf16[1,768,2304]{2,0,1:T(2,128)(2,1)} async-done(((bf16[1,6,2304]{2,0,1:T(2,128)(2,1)}), bf16[1,768,2304]{2,0,1:T(2,128)(2,1)}) %all-gather.21.cloned.1.call-update) | async-done | bytes 3538960 | tf_op jit(solution)/shard_map/all_gather | solution.py:127
  93.2 42.5 %all-gather.13.cloned.1.call-done = bf16[4096,768]{1,0:T(8,128)(2,1)} async-done(((bf16[128,768]{1,0:T(8,128)(2,1)}), bf16[4096,768]{1,0:T(8,128)(2,1)}) %all-gather.13.cloned.1.call-update) | async-done | bytes 6291472 | tf_op jit(solution)/shard_map/all_gather | solution.py:198
  135.7 8.6 copy.233
  144.3 7.1 copy.291
  156.3 29.8 %all-gather.15.cloned.1.call-done = bf16[4096,768]{1,0:T(8,128)(2,1)} async-done(((bf16[128,768]{1,0:T(8,128)(2,1)}), bf16[4096,768]{1,0:T(8,128)(2,1)}) %all-gather.15.cloned.1.call-update) | async-done | bytes 6291472 | tf_op jit(solution)/shard_map/all_gather | solution.py:197
  186.1 8.9 copy.234
  207.0 28.8 %while.50 = (s32[]{:T(128)}, f32[12,128]{1,0:T(8,128)S(1)}, f32[12,128]{1,0:T(8,128)S(1)}, s32[8,512]{1,0:T(8,128)}, s32[128]{0:T(128)S(1)}, /*index=5*/bf16[8,5...) while((s32[]{:T(128)}, f32[12,128]{1,0:T(8,128)S(1)}, ...), condition=%wide.region_7.8_spmd.clone, body=%wide.region_4.7_spmd.clone.sunk | while | flops 107027968 | bytes 7557752 | solution.py:163
  236.4 56.7 %while.51 = (s32[]{:T(128)}, f32[128,12,64]{0,2,1:T(8,128)S(1)}, f32[128,12,64]{0,2,1:T(8,128)S(1)}, bf16[8,512,12,64]{1,3,2,0:T(8,128)(2,1)}, s32[8,512]{1,0:T(...) while((s32[]{:T(128)}, f32[128,12,64]{0,2,1:T(8,128)S(1)}, ...), condition=%wide.region_9.10_spmd.clone, body=%wide.region_8.9_spmd.clone.sunk | while | flops 311099392 | bytes 13785744 | solution.py:191
  296.3 29.2 %all-gather.25.cloned.1.call-done = bf16[1,768,3072]{2,0,1:T(2,128)(2,1)} async-done(((bf16[1,6,3072]{2,0,1:T(2,128)(2,1)}), bf16[1,768,3072]{2,0,1:T(2,128)(2,1)}) %all-gather.25.cloned.1.call-update) | async-done | bytes 4718608 | tf_op jit(solution)/shard_map/all_gather | solution.py:129
  331.0 66.3 %all-gather.27.cloned.1.call-done = bf16[1,768,3072]{2,0,1:T(2,128)(2,1)} async-done(((bf16[1,6,3072]{2,0,1:T(2,128)(2,1)}), bf16[1,768,3072]{2,0,1:T(2,128)(2,1)}) %all-gather.27.cloned.1.call-update) | async-done | bytes 4718608 | tf_op jit(solution)/shard_map/all_gather | solution.py:130
  397.3 7.0 convert_reduce_fusion
  412.5 33.9 %all-gather.17.cloned.1.call-done = bf16[4096,768]{1,0:T(8,128)(2,1)} async-done(((bf16[128,768]{1,0:T(8,128)(2,1)}), bf16[4096,768]{1,0:T(8,128)(2,1)}) %all-gather.17.cloned.1.call-update) | async-done | bytes 6291472 | tf_op jit(solution)/shard_map/all_gather | solution.py:352
  446.4 8.7 copy.242
  455.1 7.1 copy.293
  467.2 23.7 %all_gather.40 = f32[4096,12]{0,1:T(8,128)S(1)} all-gather(f32[128,12]{0,1:T(8,128)} %bitcast.10), channel_id=1, replica_groups=mesh['ctx'=32,'wsh'=4] {'ctx'}, dimensions={0}, use_global_device_ids=true | all-gather | bytes 202752 | tf_op jit(solution)/shard_map/all_gather | solution.py:311
  493.4 23.1 %all_gather.42 = f32[4096,12]{0,1:T(8,128)S(1)} all-gather(f32[128,12]{0,1:T(8,128)} %multiply_reduce_fusion.1), channel_id=1, replica_groups=mesh['ctx'=32,'wsh'=4] {'ctx'}, dimensions={0}, use_global_device_ids=true | all-gather | bytes 202752 | tf_op jit(solution)/shard_map/all_gather | solution.py:312
  517.4 56.6 %while.52 = (s32[]{:T(128)}, f32[128,12,64]{0,2,1:T(8,128)}, bf16[8,512,12,64]{1,3,2,0:T(8,128)(2,1)}, s32[8,512]{1,0:T(8,128)}, s32[128]{0:T(128)S(1)}, /*index...) while((s32[]{:T(128)}, f32[128,12,64]{0,2,1:T(8,128)}, ...), condition=%wide.region_16.17_spmd.clone, body=%wide.region_15.16_spmd.clone.sunk | while | flops 306970624 | bytes 9986190 | solution.py:299
  591.4 8.8 copy.244
  600.2 7.0 copy.295
  612.1 107.0 %while.53 = (s32[]{:T(128)}, f32[128,12,64]{0,2,1:T(8,128)}, f32[128,12,64]{0,2,1:T(8,128)}, bf16[8,512,12,64]{1,3,2,0:T(8,128)(2,1)}, s32[128]{0:T(128)S(1)}, /...) while((s32[]{:T(128)}, f32[128,12,64]{0,2,1:T(8,128)}, ...), condition=%wide.region_18.19_spmd.clone, body=%wide.region_17.18_spmd.clone.sunk | while | flops 410976256 | bytes 15048863 | solution.py:347
  726.4 19.4 %pad_maximum_fusion = f32[768,9216]{1,0:T(8,128)} fusion(f32[768,3072]{1,0:T(8,128)} %convolution_bitcast_fusion, f32[768,3072]{1,0:T(8,128)} %fusion.190, f32[768,768]{1,0:T(8,128)S(1)} %copy-done, f32[768,2304]{1,0:T(8,128)} %fusion.154), kind=kLoop, calls=%fused_computation.96 | loop fusion | flops 21233664 | bytes 56623104 | tf_op jit(solution)/shard_map/concatenate | solution.py:64
  745.9 414.1 %fusion = f32[8,9216]{1,0:T(8,128)S(1)} fusion(f32[768,9216]{1,0:T(8,128)} %pad_maximum_fusion), kind=kCustom, calls=%all-reduce-scatter | all-reduce-scatter fusion | flops 9437185 | bytes 28606464
  1191.8 7.5 collective-permute-start.22
  1231.9 10.8 collective-permute-start.16
  1242.8 13.2 collective-permute-start.15
  1264.7 7.7 collective-permute-start.13
  1287.6 10.5 collective-permute-start.9
  1300.4 9.7 collective-permute-start.7
  1310.1 16.0 %collective-permute-done.11 = f32[8,9216]{1,0:T(8,128)S(1)} collective-permute-done((f32[8,9216]{1,0:T(8,128)S(1)}, f32[8,9216]{1,0:T(8,128)S(1)}, u32[]{:S(2)}, u32[]{:S(2)}) %collective-permute-start.11) | collective-permute-done | bytes 294944
  1330.2 8.5 collective-permute-start.4
  1356.4 80.2 %psum.7 = f32[1,12,768]{2,0,1:T(1,128)S(1)} all-reduce(f32[1,12,768]{2,0,1:T(1,128)S(1)} %stack.27), channel_id=1, replica_groups=mesh['ctx'=32,'wsh'=4] {'ctx','wsh'}, use_global_device_ids=true, to_apply=%region_31.32 | all-reduce | flops 9216 | bytes 73728 | tf_op jit(solution)/shard_map/psum | solution.py:396
  1437.7 137.0 %concatenate.12 = f32[262,9216]{1,0:T(8,128)} concatenate(f32[6,9216]{1,0:T(8,128)S(1)} %copy-done.34, f32[8,9216]{1,0:T(8,128)S(1)} %copy-done.32, f32[8,9216]{1,0:T(8,128)S(1)} %copy-done.36, f32[8,9216]{1,0:T(8,128)S(1)} %copy-done.38, f32[8,9216]{1,0:T(8,128)S(1)} %copy-done.40, f32[8,9216]{1,0:T(8,128)S(1)} %copy-done.42, f32[8,9216]{1,0:T(8,128)} %copy-done.43, ...), dimensions={0} | concatenate | bytes 19316736
  (556 shorter events, 455.2 us)
Async XLA Ops:
  7.2 77.0 %all-gather.21.cloned.1.call-start = ((), (), s32[]{:S(2)}) async-start(), calls=%async_computation.4 | async-start | bytes 7133184 | tf_op jit(solution)/shard_map/all_gather | solution.py:127
  8.7 127.0 %all-gather.13.cloned.1.call-start = ((), (), s32[]{:S(2)}) async-start(), calls=%async_computation | async-start | bytes 6488064 | tf_op jit(solution)/shard_map/all_gather | solution.py:198
  88.9 97.3 %all-gather.15.cloned.1.call-start = ((), (), s32[]{:S(2)}) async-start(), calls=%async_computation.1 | async-start | bytes 6488064 | tf_op jit(solution)/shard_map/all_gather | solution.py:197
  89.6 203.6 %all-gather.23.cloned.1.call-start = ((), (), s32[]{:S(2)}) async-start(), calls=%async_computation.5 | async-start | bytes 2377728 | tf_op jit(solution)/shard_map/all_gather | solution.py:128
  90.3 235.1 %all-gather.25.cloned.1.call-start = ((), (), s32[]{:S(2)}) async-start(), calls=%async_computation.6 | async-start | bytes 9510912 | tf_op jit(solution)/shard_map/all_gather | solution.py:129
  91.1 306.2 %all-gather.27.cloned.1.call-start = ((), (), s32[]{:S(2)}) async-start(), calls=%async_computation.7 | async-start | bytes 9510912 | tf_op jit(solution)/shard_map/all_gather | solution.py:130
  91.9 354.5 %all-gather.17.cloned.1.call-start = ((), (), s32[]{:S(2)}) async-start(), calls=%async_computation.2 | async-start | bytes 6488064 | tf_op jit(solution)/shard_map/all_gather | solution.py:352
  93.1 498.2 %all-gather.19.cloned.1.call-start = ((), (), s32[]{:S(2)}) async-start(), calls=%async_computation.3 | async-start | bytes 6488064 | tf_op jit(solution)/shard_map/all_gather | solution.py:353
  1179.2 26.6 %collective-permute-start.25 = (f32[8,9216]{1,0:T(8,128)S(1)}, f32[8,9216]{1,0:T(8,128)S(1)}, u32[]{:S(2)}, u32[]{:S(2)}) collective-permute-start(f32[8,9216]{1,0:T(8,128)S(1)} %fusion), channel_id=1, source_target_pairs={{0,26},{1,27},{2,28},{3,29},{4,30},{5,31},{6,32},{7,33},{8,34},{9,... | collective-permute-start | bytes 884744
  1185.0 28.5 %collective-permute-start.24 = (f32[8,9216]{1,0:T(8,128)S(1)}, f32[8,9216]{1,0:T(8,128)}, u32[]{:S(2)}, u32[]{:S(2)}) collective-permute-start(f32[8,9216]{1,0:T(8,128)S(1)} %fusion), channel_id=1, source_target_pairs={{0,25},{1,26},{2,27},{3,28},{4,29},{5,30},{6,31},{7,32},{8,33},{9,... | collective-permute-start | bytes 884744
  1187.6 31.3 %collective-permute-start.23 = (f32[8,9216]{1,0:T(8,128)S(1)}, f32[8,9216]{1,0:T(8,128)}, u32[]{:S(2)}, u32[]{:S(2)}) collective-permute-start(f32[8,9216]{1,0:T(8,128)S(1)} %fusion), channel_id=1, source_target_pairs={{0,24},{1,25},{2,26},{3,27},{4,28},{5,29},{6,30},{7,31},{8,32},{9,... | collective-permute-start | bytes 884744
  1191.8 33.9 %collective-permute-start.22 = (f32[8,9216]{1,0:T(8,128)S(1)}, f32[8,9216]{1,0:T(8,128)}, u32[]{:S(2)}, u32[]{:S(2)}) collective-permute-start(f32[8,9216]{1,0:T(8,128)S(1)} %fusion), channel_id=1, source_target_pairs={{0,23},{1,24},{2,25},{3,26},{4,27},{5,28},{6,29},{7,30},{8,31},{9,... | collective-permute-start | bytes 884744
  1199.3 32.6 %collective-permute-start.21 = (f32[8,9216]{1,0:T(8,128)S(1)}, f32[8,9216]{1,0:T(8,128)}, u32[]{:S(2)}, u32[]{:S(2)}) collective-permute-start(f32[8,9216]{1,0:T(8,128)S(1)} %fusion), channel_id=1, source_target_pairs={{0,22},{1,23},{2,24},{3,25},{4,26},{5,27},{6,28},{7,29},{8,30},{9,... | collective-permute-start | bytes 884744
  1205.9 36.9 %collective-permute-start.20 = (f32[8,9216]{1,0:T(8,128)S(1)}, f32[8,9216]{1,0:T(8,128)}, u32[]{:S(2)}, u32[]{:S(2)}) collective-permute-start(f32[8,9216]{1,0:T(8,128)S(1)} %fusion), channel_id=1, source_target_pairs={{0,21},{1,22},{2,23},{3,24},{4,25},{5,26},{6,27},{7,28},{8,29},{9,... | collective-permute-start | bytes 884744
  1213.5 49.2 %collective-permute-start.19 = (f32[8,9216]{1,0:T(8,128)S(1)}, f32[8,9216]{1,0:T(8,128)S(1)}, u32[]{:S(2)}, u32[]{:S(2)}) collective-permute-start(f32[8,9216]{1,0:T(8,128)S(1)} %fusion), channel_id=1, source_target_pairs={{0,20},{1,21},{2,22},{3,23},{4,24},{5,25},{6,26},{7,27},{8,28},{9,... | collective-permute-start | bytes 884744
  1218.9 45.7 %collective-permute-start.18 = (f32[8,9216]{1,0:T(8,128)S(1)}, f32[8,9216]{1,0:T(8,128)S(1)}, u32[]{:S(2)}, u32[]{:S(2)}) collective-permute-start(f32[8,9216]{1,0:T(8,128)S(1)} %fusion), channel_id=1, source_target_pairs={{0,19},{1,20},{2,21},{3,22},{4,23},{5,24},{6,25},{7,26},{8,27},{9,... | collective-permute-start | bytes 884744
  1225.6 46.8 %collective-permute-start.17 = (f32[8,9216]{1,0:T(8,128)S(1)}, f32[8,9216]{1,0:T(8,128)S(1)}, u32[]{:S(2)}, u32[]{:S(2)}) collective-permute-start(f32[8,9216]{1,0:T(8,128)S(1)} %fusion), channel_id=1, source_target_pairs={{0,18},{1,19},{2,20},{3,21},{4,22},{5,23},{6,24},{7,25},{8,26},{9,... | collective-permute-start | bytes 884744
  1231.9 46.3 %collective-permute-start.16 = (f32[8,9216]{1,0:T(8,128)S(1)}, f32[8,9216]{1,0:T(8,128)S(1)}, u32[]{:S(2)}, u32[]{:S(2)}) collective-permute-start(f32[8,9216]{1,0:T(8,128)S(1)} %fusion), channel_id=1, source_target_pairs={{0,17},{1,18},{2,19},{3,20},{4,21},{5,22},{6,23},{7,24},{8,25},{9,... | collective-permute-start | bytes 884744
  1242.8 37.4 %collective-permute-start.15 = (f32[8,9216]{1,0:T(8,128)S(1)}, f32[8,9216]{1,0:T(8,128)S(1)}, u32[]{:S(2)}, u32[]{:S(2)}) collective-permute-start(f32[8,9216]{1,0:T(8,128)S(1)} %fusion), channel_id=1, source_target_pairs={{0,16},{1,17},{2,18},{3,19},{4,20},{5,21},{6,22},{7,23},{8,24},{9,... | collective-permute-start | bytes 884744
  1262.7 24.9 %collective-permute-start.14 = (f32[8,9216]{1,0:T(8,128)S(1)}, f32[8,9216]{1,0:T(8,128)S(1)}, u32[]{:S(2)}, u32[]{:S(2)}) collective-permute-start(f32[8,9216]{1,0:T(8,128)S(1)} %fusion), channel_id=1, source_target_pairs={{0,15},{1,16},{2,17},{3,18},{4,19},{5,20},{6,21},{7,22},{8,23},{9,... | collective-permute-start | bytes 884744
  1264.7 33.4 %collective-permute-start.13 = (f32[8,9216]{1,0:T(8,128)S(1)}, f32[8,9216]{1,0:T(8,128)S(1)}, u32[]{:S(2)}, u32[]{:S(2)}) collective-permute-start(f32[8,9216]{1,0:T(8,128)S(1)} %fusion), channel_id=1, source_target_pairs={{0,14},{1,15},{2,16},{3,17},{4,18},{5,19},{6,20},{7,21},{8,22},{9,... | collective-permute-start | bytes 884744
  1272.4 27.9 %collective-permute-start.12 = (f32[8,9216]{1,0:T(8,128)S(1)}, f32[8,9216]{1,0:T(8,128)S(1)}, u32[]{:S(2)}, u32[]{:S(2)}) collective-permute-start(f32[8,9216]{1,0:T(8,128)S(1)} %fusion), channel_id=1, source_target_pairs={{0,13},{1,14},{2,15},{3,16},{4,17},{5,18},{6,19},{7,20},{8,21},{9,... | collective-permute-start | bytes 884744
  1278.3 47.8 %collective-permute-start.11 = (f32[8,9216]{1,0:T(8,128)S(1)}, f32[8,9216]{1,0:T(8,128)S(1)}, u32[]{:S(2)}, u32[]{:S(2)}) collective-permute-start(f32[8,9216]{1,0:T(8,128)S(1)} %fusion), channel_id=1, source_target_pairs={{0,12},{1,13},{2,14},{3,15},{4,16},{5,17},{6,18},{7,19},{8,20},{9,... | collective-permute-start | bytes 884744
  1280.2 47.2 %collective-permute-start.10 = (f32[8,9216]{1,0:T(8,128)S(1)}, f32[8,9216]{1,0:T(8,128)S(1)}, u32[]{:S(2)}, u32[]{:S(2)}) collective-permute-start(f32[8,9216]{1,0:T(8,128)S(1)} %fusion), channel_id=1, source_target_pairs={{0,11},{1,12},{2,13},{3,14},{4,15},{5,16},{6,17},{7,18},{8,19},{9,... | collective-permute-start | bytes 884744
  1287.6 42.5 %collective-permute-start.9 = (f32[8,9216]{1,0:T(8,128)S(1)}, f32[8,9216]{1,0:T(8,128)S(1)}, u32[]{:S(2)}, u32[]{:S(2)}) collective-permute-start(f32[8,9216]{1,0:T(8,128)S(1)} %fusion), channel_id=1, source_target_pairs={{0,10},{1,11},{2,12},{3,13},{4,14},{5,15},{6,16},{7,17},{8,18},{9,... | collective-permute-start | bytes 884744
  1298.1 40.6 %collective-permute-start.8 = (f32[8,9216]{1,0:T(8,128)S(1)}, f32[8,9216]{1,0:T(8,128)S(1)}, u32[]{:S(2)}, u32[]{:S(2)}) collective-permute-start(f32[8,9216]{1,0:T(8,128)S(1)} %fusion), channel_id=1, source_target_pairs={{0,9},{1,10},{2,11},{3,12},{4,13},{5,14},{6,15},{7,16},{8,17},{9,1... | collective-permute-start | bytes 884744
  1300.4 44.7 %collective-permute-start.7 = (f32[8,9216]{1,0:T(8,128)S(1)}, f32[8,9216]{1,0:T(8,128)S(1)}, u32[]{:S(2)}, u32[]{:S(2)}) collective-permute-start(f32[8,9216]{1,0:T(8,128)S(1)} %fusion), channel_id=1, source_target_pairs={{0,8},{1,9},{2,10},{3,11},{4,12},{5,13},{6,14},{7,15},{8,16},{9,17... | collective-permute-start | bytes 884744
  1330.2 107.4 %collective-permute-start.4 = (f32[8,9216]{1,0:T(8,128)S(1)}, f32[8,9216]{1,0:T(8,128)}, u32[]{:S(2)}, u32[]{:S(2)}) collective-permute-start(f32[8,9216]{1,0:T(8,128)S(1)} %fusion), channel_id=1, source_target_pairs={{0,5},{1,6},{2,7},{3,8},{4,9},{5,10},{6,11},{7,12},{8,13},{9,14},{... | collective-permute-start | bytes 884744
  1338.7 98.9 %collective-permute-start.3 = (f32[8,9216]{1,0:T(8,128)S(1)}, f32[8,9216]{1,0:T(8,128)}, u32[]{:S(2)}, u32[]{:S(2)}) collective-permute-start(f32[8,9216]{1,0:T(8,128)S(1)} %fusion), channel_id=1, source_target_pairs={{0,4},{1,5},{2,6},{3,7},{4,8},{5,9},{6,10},{7,11},{8,12},{9,13},{1... | collective-permute-start | bytes 884744
  1345.1 92.5 %collective-permute-start.2 = (f32[8,9216]{1,0:T(8,128)S(1)}, f32[8,9216]{1,0:T(8,128)}, u32[]{:S(2)}, u32[]{:S(2)}) collective-permute-start(f32[8,9216]{1,0:T(8,128)S(1)} %fusion), channel_id=1, source_target_pairs={{0,3},{1,4},{2,5},{3,6},{4,7},{5,8},{6,9},{7,10},{8,11},{9,12},{10... | collective-permute-start | bytes 884744
  1347.0 90.6 %collective-permute-start.1 = (f32[8,9216]{1,0:T(8,128)S(1)}, f32[8,9216]{1,0:T(8,128)}, u32[]{:S(2)}, u32[]{:S(2)}) collective-permute-start(f32[8,9216]{1,0:T(8,128)S(1)} %fusion), channel_id=1, source_target_pairs={{0,2},{1,3},{2,4},{3,5},{4,6},{5,7},{6,8},{7,9},{8,10},{9,11},{10,... | collective-permute-start | bytes 884744
  1349.7 87.9 %collective-permute-start = (f32[8,9216]{1,0:T(8,128)S(1)}, f32[8,9216]{1,0:T(8,128)}, u32[]{:S(2)}, u32[]{:S(2)}) collective-permute-start(f32[8,9216]{1,0:T(8,128)S(1)} %fusion), channel_id=1, source_target_pairs={{0,1},{1,2},{2,3},{3,4},{4,5},{5,6},{6,7},{7,8},{8,9},{9,10},{10,1... | collective-permute-start | bytes 884744
  (106 other events, 10166.3 us)
Sparse Core Ops, SparseCore 0:
  11.6 72.6 all-gather.20
  89.0 46.6 all-gather.12
  138.0 48.1 all-gather.14
  189.5 64.1 all-gather.22
  257.2 68.2 all-gather.24
  328.9 68.3 all-gather.26
  399.6 46.7 all-gather.16
  448.6 48.9 all-gather.18
where the time goes:
time: 1610 us; the launch traced here: 1590 us
  blocking collectives  541 us (34%)
  waiting for transfers between devices  295 us (18%)
  local copies, waits for them, and re-layouts  284 us (18%)
  matrix products  236 us (15%)
  starting transfers between devices  159 us (10%)
  other arithmetic  57.7 us (4%)
    unnamed x1, blocking collectives  414 us
    unnamed x218, local copies, waits for them, and re-layouts  197 us
    unnamed x32, starting transfers between devices  159 us
    psum x1, blocking collectives, local(): vector_total = lax.psum(jnp.stack(vector_grads, axis=0), ('ctx', 'wsh'))  80.2 us
    all_gather x1, waiting for transfers between devices, local(): lax.all_gather(mix_part, ('ctx', 'wsh'), axis=0, tiled=True)  71.8 us
    all_gather x1, waiting for transfers between devices, local(): lax.all_gather(down_part, ('ctx', 'wsh'), axis=0, tiled=True)  66.3 us
    dot_general x32, matrix products, head_scores(): jnp.einsum('qhd,khd->hqk', query_part, key_part, preferred_element_type=j...  58 us
    all_gather x1, waiting for transfers between devices, local(): lax.all_gather(value_rows, 'ctx', axis=0, tiled=True)  42.5 us
  transfers between devices with their start and end apart: 40, of which 9 were waited for; matrix products, arithmetic and copies ran while one was open for 17% of the time, Pallas kernels for 0%

commit v1 on v0

v1 whole, which is shorter than its diff:
```python
import jax
import jax.numpy as jnp
import numpy as np
from jax import lax
from jax.experimental import pallas as pl
from jax.experimental.pallas import tpu as pltpu
from jax.sharding import Mesh
from jax.sharding import PartitionSpec as P

D = 768
HEADS = 12
HD = 64
FF = 3072
LAYERS = 1
STEP = 5

EPS_NORM = 1e-05
NEGATIVE = -1e30
BETA_ONE = 0.9
BETA_TWO = 0.999
RATE_MATRIX = 0.1
RATE_VECTOR = 0.5
DECAY_MATRIX = 0.1
EPS_ADAM = 1e-08

NX = 4
NZ = 4
NC = 2
NY = 4
GH = HEADS // NX
GD = GH * HD
ROWS = 128
BLK = 64
QROWS = NX * ROWS
SEQ = 4096
NBLK = SEQ // BLK
CHUNK = 1024
GB = 4
WAYS = BLK * GB
BF = jnp.bfloat16
F32 = jnp.float32
VMEM = pltpu.VMEM
SMEM = pltpu.SMEM


def layer_norm(hidden, norm_gain, norm_shift):
    center = hidden - jnp.mean(hidden, axis=-1, keepdims=True)
    spread = jnp.mean(center * center, axis=-1, keepdims=True)
    return center * lax.rsqrt(spread + EPS_NORM) * norm_gain + norm_shift


def adamw(weight, moment, second, gradient, step_rate, decay_rate):
    moment_new = BETA_ONE * moment + (1.0 - BETA_ONE) * gradient
    second_new = BETA_TWO * second + (1.0 - BETA_TWO) * gradient * gradient
    moment_hat = moment_new / (1.0 - BETA_ONE**STEP)
    second_hat = second_new / (1.0 - BETA_TWO**STEP)
    weight_new = weight - step_rate * (
        moment_hat / (jnp.sqrt(second_hat) + EPS_ADAM) + decay_rate * weight
    )
    return (moment_new, second_new, weight_new)


RIGHT = [(i, (i + 1) % 4) for i in range(4)]
LEFT = [(i, (i + 3) % 4) for i in range(4)]
SWAP = [(0, 1), (1, 0)]
EVEN = [(0, 1), (1, 0), (2, 3), (3, 2)]
ODD = [(1, 2), (2, 1), (3, 0), (0, 3)]


def ring_gather(part, axis):
    half = part.shape[0] // 2
    before = lax.ppermute(part, axis, RIGHT)
    after = lax.ppermute(part, axis, LEFT)
    far_low = lax.ppermute(before[:half], axis, RIGHT)
    far_high = lax.ppermute(after[half:], axis, LEFT)
    return jnp.concatenate([part, before, after, far_low, far_high], axis=0)


def ordered(gathered, axis):
    rows = gathered.shape[0] // 4
    me = lax.axis_index(axis)
    relative = lax.rem(4 + jnp.arange(4) - me, 4)
    slot = jnp.where(relative == 1, 2, jnp.where(relative == 2, 3, jnp.where(relative == 3, 1, 0)))
    return jnp.take(gathered.reshape(4, rows, -1), slot, axis=0).reshape(gathered.shape)


def gather_zc(part):
    own = ring_gather(part, "z")
    return own, lax.ppermute(own, "c", SWAP)


def copy_gather(part, axes):
    count = lax.axis_size(axes)
    return lax.all_to_all(jnp.broadcast_to(part[None], (count,) + part.shape), axes, 0, 0, tiled=True)


def widening():
    pick = np.zeros((D, 8 * 128), np.float32)
    feature = np.arange(D)
    pick[feature, feature // 6 * 8 + feature % 6] = 1.0
    return pick


def filling(part):
    pick = np.zeros((D, 8 * 128), np.float32)
    device = np.arange(128)
    pick[6 * device + part, 8 * device + 6] = 1.0
    pick[6 * device + 3 + part, 8 * device + 7] = 1.0
    return pick


def dot_nt(left, right):
    return lax.dot_general(left, right, (((1,), (1,)), ((), ())), preferred_element_type=F32)


def dot_nn(left, right):
    return lax.dot_general(left, right, (((1,), (0,)), ((), ())), preferred_element_type=F32)


def group_rows(ref, blocks, columns):
    return jnp.concatenate(
        [ref[pl.ds(pl.multiple_of(block * BLK, BLK), BLK), columns] for block in blocks], axis=0
    )


def store_group(ref, blocks, columns, value):
    for at, block in enumerate(blocks):
        rows = slice(at * BLK, (at + 1) * BLK)
        ref[pl.ds(pl.multiple_of(block * BLK, BLK), BLK), columns] = value[rows]


def group_places(blocks, shape, axis):
    index = lax.broadcasted_iota(jnp.int32, shape, axis)
    places = blocks[0] * BLK + index
    for at in range(1, len(blocks)):
        places = jnp.where(index < at * BLK, places, (blocks[at] - at) * BLK + index)
    return places


def group_of(tab, g):
    own = [tab[NBLK + GB * g + j] for j in range(GB)]
    return own, [tab[NBLK + 8 + GB * g + j] for j in range(GB)]


def sort_blocks(tab, sources, store, at=0):
    for source in sources:
        count = source.shape[0] // BLK

        def move(block, carry, source=source, at=at):
            place = tab[at + block]
            rows = source[pl.ds(pl.multiple_of(block * BLK, BLK), BLK), :]
            store(pl.multiple_of(place * BLK, BLK), rows)
            return carry

        lax.fori_loop(0, count, move, 0)
        at = at + count


def head_columns(head, part=0):
    return slice(part * GD + head * HD, part * GD + (head + 1) * HD)


def forward_kernel(tab, q, kv_own, kv_other, att, exact, stats, k_s, v_s):
    def store(at, rows):
        ones = jnp.ones((BLK, HD), BF)
        for head in range(GH):
            k_s[head, pl.ds(at, BLK), :] = rows[:, head_columns(head)]
            v_s[head, pl.ds(at, BLK), :] = jnp.concatenate(
                [rows[:, head_columns(head, 1)], ones], axis=1
            )

    sort_blocks(tab, (kv_own, kv_other), store)
    lane = lax.broadcasted_iota(jnp.int32, (WAYS, 128), 1)

    def group(g, carry):
        own, at_places = group_of(tab, g)
        places = group_places(at_places, (WAYS, 1), 0)
        queries = [
            group_rows(q, own, head_columns(h)) * jnp.asarray(0.125, BF)
            for h in range(GH)
        ]

        def chunk(at, state):
            start = pl.multiple_of(at * CHUNK, CHUNK)
            keys_at = start + lax.broadcasted_iota(jnp.int32, (WAYS, CHUNK), 1)
            allowed = keys_at <= places
            out = []
            for h in range(GH):
                peak, plain, extra = state[h]
                scores = dot_nt(queries[h], k_s[h, pl.ds(start, CHUNK), :])
                scores = jnp.where(allowed, scores, NEGATIVE)
                peak_new = jnp.maximum(peak, jnp.max(scores, axis=1, keepdims=True))
                shrink = jnp.exp(peak - peak_new)
                expo = jnp.exp(scores - peak_new)
                probs = expo.astype(BF)
                residue = (expo - probs.astype(F32)).astype(BF)
                values = v_s[h, pl.ds(start, CHUNK), :]
                plain = plain * shrink + dot_nn(probs, values)
                extra = extra * shrink + dot_nn(residue, values)
                out.append((peak_new, plain, extra))
            return tuple(out)

        zero = jnp.zeros((WAYS, 128), F32)
        begin = tuple((jnp.full((WAYS, 1), NEGATIVE, F32), zero, zero) for _ in range(GH))
        state = lax.fori_loop(0, lax.div(at_places[-1], CHUNK // BLK) + 1, chunk, begin)
        table = jnp.zeros((WAYS, 128), F32)
        for h in range(GH):
            peak, plain, extra = state[h]
            both = plain + extra
            mass = both[:, HD : HD + 1]
            store_group(att, own, head_columns(h), (plain[:, :HD] / mass).astype(BF))
            store_group(exact, own, head_columns(h), both[:, :HD] / mass)
            table = jnp.where(lane == h, peak + jnp.log(mass), table)
        store_group(stats, own, slice(0, 128), table)
        return carry

    lax.fori_loop(0, 8 // GB, group, 0)


def pack_kernel(back, exact, stats_in, packed, stats):
    lane = lax.broadcasted_iota(jnp.int32, (QROWS, 128), 1)
    table = stats_in[...]
    extra = jnp.zeros((QROWS, 128), F32)
    for h in range(GH):
        columns = head_columns(h)
        dot = jnp.sum(back[:, columns].astype(F32) * exact[:, columns], axis=1, keepdims=True)
        table = jnp.where(lane == GH + h, dot, table)
    stats[...] = table
    for j in range(2 * GH):
        value = table[:, j : j + 1]
        for t in range(3):
            piece = value.astype(BF).astype(F32)
            value = value - piece
            extra = jnp.where(lane == 3 * j + t, piece, extra)
    packed[:, :GD] = back[...]
    packed[:, GD:] = extra[:, : 256 - GD].astype(BF)


def query_kernel(tab, q, back, stats, kv_own, kv_other, grad, k_s, v_s):
    def store(at, rows):
        for head in range(GH):
            k_s[head, pl.ds(at, BLK), :] = rows[:, head_columns(head)]
            v_s[head, pl.ds(at, BLK), :] = rows[:, head_columns(head, 1)]

    sort_blocks(tab, (kv_own, kv_other), store)

    def group(g, carry):
        own, at_places = group_of(tab, g)
        places = group_places(at_places, (WAYS, 1), 0)
        table = group_rows(stats, own, slice(0, 128))
        queries = [
            group_rows(q, own, head_columns(h)) * jnp.asarray(0.125, BF)
            for h in range(GH)
        ]
        backs = [group_rows(back, own, head_columns(h)) for h in range(GH)]

        def chunk(at, state):
            start = pl.multiple_of(at * CHUNK, CHUNK)
            keys_at = start + lax.broadcasted_iota(jnp.int32, (WAYS, CHUNK), 1)
            allowed = keys_at <= places
            out = []
            for h in range(GH):
                keys = k_s[h, pl.ds(start, CHUNK), :]
                scores = dot_nt(queries[h], keys) - table[:, h : h + 1]
                expo = jnp.exp(jnp.where(allowed, scores, NEGATIVE))
                dots = dot_nt(backs[h], v_s[h, pl.ds(start, CHUNK), :])
                slopes = (expo * (dots - table[:, GH + h : GH + h + 1])).astype(BF)
                out.append(state[h] + dot_nn(slopes, keys))
            return tuple(out)

        begin = tuple(jnp.zeros((WAYS, HD), F32) for _ in range(GH))
        state = lax.fori_loop(0, lax.div(at_places[-1], CHUNK // BLK) + 1, chunk, begin)
        for h in range(GH):
            store_group(grad, own, head_columns(h), (state[h] * 0.125).astype(BF))
        return carry

    lax.fori_loop(0, 8 // GB, group, 0)


def key_kernel(tab, kv, q_all, x_all, pick, grad, q_s, d_s, r_s, row_s):
    def store_q(at, rows):
        for head in range(GH):
            q_s[head, pl.ds(at, BLK), :] = rows[:, head_columns(head)] * jnp.asarray(0.125, BF)

    def store_x(at, rows):
        for head in range(GH):
            d_s[head, pl.ds(at, BLK), :] = rows[:, head_columns(head)]
        r_s[pl.ds(at, BLK), :] = rows[:, 128:256]

    sort_blocks(tab, (q_all,), store_q, NBLK + 16)
    sort_blocks(tab, (x_all,), store_x, NBLK + 16)

    def rows_of(at, carry):
        start = pl.multiple_of(at * CHUNK, CHUNK)
        row_s[at] = dot_nt(pick[...], r_s[pl.ds(start, CHUNK), :])
        return carry

    lax.fori_loop(0, SEQ // CHUNK, rows_of, 0)

    def group(g, carry):
        own, at_places = group_of(tab, g)
        places = group_places(at_places, (WAYS, 1), 0)
        keys = [group_rows(kv, own, head_columns(h)) for h in range(GH)]
        values = [group_rows(kv, own, head_columns(h, 1)) for h in range(GH)]

        def chunk(at, state):
            start = pl.multiple_of(at * CHUNK, CHUNK)
            queries_at = start + lax.broadcasted_iota(jnp.int32, (WAYS, CHUNK), 1)
            allowed = places <= queries_at
            rows = row_s[at]
            out = []
            for h in range(GH):
                queries = q_s[h, pl.ds(start, CHUNK), :]
                backs = d_s[h, pl.ds(start, CHUNK), :]
                scores = dot_nt(keys[h], queries) - rows[h : h + 1, :]
                expo = jnp.exp(jnp.where(allowed, scores, NEGATIVE))
                dots = dot_nt(values[h], backs)
                slopes = (expo * (dots - rows[GH + h : GH + h + 1, :])).astype(BF)
                key_grad, value_grad = state[h]
                out.append(
                    (
                        key_grad + dot_nn(slopes, queries),
                        value_grad + dot_nn(expo.astype(BF), backs),
                    )
                )
            return tuple(out)

        zero = jnp.zeros((WAYS, HD), F32)
        begin = tuple((zero, zero) for _ in range(GH))
        state = lax.fori_loop(lax.div(at_places[0], CHUNK // BLK), SEQ // CHUNK, chunk, begin)
        for h in range(GH):
            store_group(grad, own, head_columns(h), state[h][0].astype(BF))
            store_group(grad, own, head_columns(h, 1), state[h][1].astype(BF))
        return carry

    lax.fori_loop(0, 8 // GB, group, 0)


def call(kernel, operands, outs, scratch, cost, tabled=True):
    specs = [pl.BlockSpec(memory_space=VMEM)] * (len(operands) - int(tabled))
    if tabled:
        specs = [pl.BlockSpec(memory_space=SMEM)] + specs
    return pl.pallas_call(
        kernel,
        in_specs=specs,
        out_specs=[pl.BlockSpec(memory_space=VMEM)] * len(outs),
        out_shape=[jax.ShapeDtypeStruct(shape, kind) for shape, kind in outs],
        scratch_shapes=scratch,
        compiler_params=pltpu.CompilerParams(vmem_limit_bytes=40 * 2**20),
        cost_estimate=pl.CostEstimate(flops=cost, bytes_accessed=8 * 2**20, transcendentals=0),
    )(*operands)


HEAD_SCRATCH = VMEM((GH, SEQ, HD), BF)


def attend(tab, q, kv_own, kv_other):
    return call(
        forward_kernel,
        (tab, q, kv_own, kv_other),
        [((QROWS, GD), BF), ((QROWS, GD), F32), ((QROWS, 128), F32)],
        [HEAD_SCRATCH, VMEM((GH, SEQ, 128), BF)],
        10**8,
    )


def pack(back, exact, stats):
    return call(
        pack_kernel,
        (back, exact, stats),
        [((QROWS, 256), BF), ((QROWS, 128), F32)],
        [],
        10**7,
        tabled=False,
    )


def query_grads(tab, q, back, stats, kv_own, kv_other):
    return call(
        query_kernel,
        (tab, q, back, stats, kv_own, kv_other),
        [((QROWS, GD), BF)],
        [HEAD_SCRATCH, HEAD_SCRATCH],
        10**8,
    )[0]


def key_grads(tab, kv, q_all, x_all):
    pick = np.zeros((8, 128), np.float32)
    for j in range(2 * GH):
        for t in range(3):
            pick[j, GD - 128 + 3 * j + t] = 1.0
    return call(
        key_kernel,
        (tab, kv, q_all.reshape(SEQ, GD), x_all.reshape(SEQ, 256), jnp.asarray(pick, BF)),
        [((QROWS, 2 * GD), BF)],
        [HEAD_SCRATCH, HEAD_SCRATCH, VMEM((SEQ, 128), BF), VMEM((SEQ // CHUNK, 8, CHUNK), F32)],
        10**8,
    )[0]


def rest_kernel(att, two, down, branch, up, active, spread_t, fill_t, grad):
    def across(table, value):
        return dot_nt(table, value).astype(BF)

    two_t, down_t = across(spread_t[...], two[...]), across(spread_t[...], down[...])
    att_t = across(spread_t[...], att[...])
    last = active[:, D:]
    tops = ((two_t, up[:, :D]), (two_t, up[:, D:]), (down_t, active[:, :D]))
    for j, (left, right) in enumerate(tops):
        left = jnp.concatenate([left, across(fill_t[j], down[...])], axis=1)
        right = jnp.concatenate([right, last], axis=0)
        grad[:, j * D : (j + 1) * D] = dot_nn(left, right).astype(BF)
    grad[:, 3 * D :] = dot_nn(att_t, branch[...]).astype(BF)


def rest_grads(*rows):
    fills = np.stack([filling(j).T for j in range(3)])
    return call(
        rest_kernel,
        (*rows, jnp.asarray(widening().T, BF), jnp.asarray(fills, BF)),
        [((8 * 128, 7 * (D // 2)), BF)],
        [],
        10**8,
        tabled=False,
    )[0]


def place_table(pair_of_device):
    z, core = lax.axis_index("z"), lax.axis_index("c")
    pairs = pair_of_device.reshape(NX, NZ, NC).transpose(1, 2, 0)
    order = jnp.stack([z, (z + 3) % 4, (z + 1) % 4, (z + 2) % 4])
    plain = jnp.stack([pairs, NBLK - 1 - pairs], axis=-1).reshape(NBLK)
    pairs = jnp.take(pairs, order, axis=0)
    pairs = jnp.stack([jnp.take(pairs, core, axis=1), jnp.take(pairs, 1 - core, axis=1)])
    blocks = jnp.stack([pairs, NBLK - 1 - pairs], axis=-1).reshape(NBLK)
    own = blocks[: 2 * NX]
    rank = jnp.sum(own[:, None] > own[None, :], axis=1)
    hit = rank[None, :] == jnp.arange(2 * NX)[:, None]
    index = jnp.sum(jnp.where(hit, jnp.arange(2 * NX)[None, :], 0), axis=1)
    place = jnp.sum(jnp.where(hit, own[None, :], 0), axis=1)
    return jnp.concatenate([blocks, index, place, plain]).astype(jnp.int32)


def local(
    tokens,
    cotangent,
    pair_of_device,
    qkv_weight,
    out_weight,
    fc1_weight,
    fc2_weight,
    vectors,
    qkv_moment,
    qkv_second,
    out_moment,
    out_second,
    fc1_moment,
    fc1_second,
    fc2_moment,
    fc2_second,
    vector_moment,
    vector_second,
):
    xi, core = lax.axis_index("x"), lax.axis_index("c")
    everyone = ("x", "z", "c", "y")
    vector = vectors[0]
    tab = place_table(pair_of_device)
    widen = jnp.asarray(widening(), BF)

    mix = qkv_weight[0].astype(BF).reshape(6, 3, NX, GD).transpose(2, 0, 1, 3).reshape(NX, 1, 6, 3 * GD)
    mix = jnp.broadcast_to(mix, (NX, NY, 6, 3 * GD)).reshape(NX * NY, 6, 3 * GD)
    mix = lax.all_to_all(mix, ("x", "y"), 0, 0, tiled=True)
    mix = copy_gather(mix.reshape(NX * NY * 6, 3 * GD), ("z", "c"))
    mix = mix.reshape(NZ, NC, NX, NY, 6, 3 * GD).transpose(2, 0, 1, 3, 4, 5)
    tokens4 = ordered(ring_gather(tokens[0], "x"), "x")

    rest = jnp.concatenate([p[0].astype(BF) for p in (out_weight, fc1_weight, fc2_weight)], axis=1)
    rest = jnp.pad(rest, ((0, 2), (0, 0)))[None]
    rest, mix, tokens4 = lax.optimization_barrier((rest, mix, tokens4))
    rest_all = lax.all_gather(rest, everyone, axis=0, tiled=True).reshape(8 * 128, D + 2 * FF)

    w_mix = mix.reshape(D, 3 * GD)

    hidden4 = tokens4.astype(F32)
    normed4 = layer_norm(hidden4, vector[0], vector[1]).astype(BF)
    projected = jnp.dot(normed4, w_mix, preferred_element_type=F32)
    group_bias = lax.dynamic_slice_in_dim(vector[2:4], xi * GD, GD, 1)
    q4 = (projected[:, :GD] + group_bias[0]).astype(BF)
    k4 = projected[:, GD : 2 * GD].astype(BF)
    v4 = (projected[:, 2 * GD :] + group_bias[1]).astype(BF)
    kv4 = jnp.concatenate([k4, v4], axis=1)
    kv_own, kv_other = gather_zc(kv4)
    q_in, _ = lax.optimization_barrier((q4, kv_other))
    q_all = copy_gather(q_in, ("z", "c"))
    att4, exact4, stats4 = attend(tab, q4, kv_own, kv_other)
    att4, q_all = lax.optimization_barrier((att4, q_all))

    attended = lax.all_to_all(att4.reshape(NX, ROWS, GD), "x", 0, 0, tiled=True)
    attended = attended.transpose(1, 0, 2).reshape(ROWS, D)

    w_out, w_up, w_down = rest_all[:, :D], rest_all[:, D : D + FF], rest_all[:, D + FF :]

    def wide(value):
        return jnp.dot(value, widen, preferred_element_type=F32).astype(BF)

    def narrow(value):
        return lax.dot_general(
            value, widen.astype(F32), (((1,), (1,)), ((), ())), precision=lax.Precision.HIGHEST
        )

    hidden = tokens[0].astype(F32)
    middle = hidden + jnp.dot(wide(attended), w_out, preferred_element_type=F32) + vector[4]
    normed_two = layer_norm(middle, vector[5], vector[6]).astype(BF)
    down_low = cotangent[0]
    back_active = jnp.dot(wide(down_low), w_down, preferred_element_type=F32)
    pre_active = jnp.dot(wide(normed_two), w_up, preferred_element_type=F32) + vector[8:12].reshape(FF)
    active_wide, gelu_back = jax.vjp(jax.nn.gelu, pre_active)
    active = active_wide.astype(BF)
    up_low = gelu_back(back_active)[0].astype(BF)
    back_two = narrow(dot_nt(up_low, w_up))

    gradient = cotangent[0].astype(F32)
    _, norm_back = jax.vjp(layer_norm, middle, vector[5], vector[6])
    back_middle, gain_two, shift_two = norm_back(back_two)
    gradient = gradient + back_middle
    branch_low = gradient.astype(BF)
    back_attended = dot_nt(branch_low, w_out).astype(BF)
    back_attended = dot_nt(back_attended, widen).astype(BF)
    back4 = lax.all_to_all(
        back_attended.reshape(ROWS, NX, GD).transpose(1, 0, 2), "x", 0, 0, tiled=True
    ).reshape(QROWS, GD)
    packed, stats_all = pack(back4, exact4, stats4)
    x_all = copy_gather(packed, ("z", "c"))

    late, _ = lax.optimization_barrier(
        ((attended, normed_two, down_low, branch_low, up_low, active), packed)
    )

    def outer(left, right):
        return jnp.einsum("rc,re->ce", left, right, preferred_element_type=F32).astype(BF)

    def half_of(value, which):
        size = value.shape[1] // 2
        return lax.dynamic_slice_in_dim(value, which * size, size, 1)

    mine = list(late[:3]) + [half_of(v, core) for v in late[3:]]
    theirs = list(late[:3]) + [half_of(v, 1 - core) for v in late[3:]]
    got = lax.ppermute(jnp.concatenate(theirs, axis=1), "c", SWAP)
    at, both = 0, []
    for value in mine:
        both.append(jnp.concatenate([value, got[:, at : at + value.shape[1]]], axis=0))
        at = at + value.shape[1]
    rest_grad = rest_grads(*both).reshape(128, 8, 7 * (D // 2))

    down_out = narrow(dot_nt(active, w_down))
    block_out = middle + down_out + vector[7]

    back_in, rest_grad = lax.optimization_barrier((back4, rest_grad))
    rest_grad = lax.all_to_all(rest_grad, everyone, 0, 0, tiled=True)
    wide4, back_in = lax.optimization_barrier((wide(normed4), back_in))
    back_q4 = query_grads(tab, q4, back_in, stats_all, kv_own, kv_other)
    back_q4, x_all = lax.optimization_barrier((back_q4, x_all))
    back_kv4 = key_grads(tab, kv4, q_all, x_all)
    back_kv4, rest_grad = lax.optimization_barrier((back_kv4, rest_grad))
    mixed4 = jnp.concatenate([back_q4, back_kv4], axis=1)

    mix_grad = outer(wide4, mixed4).reshape(128, 8, 3 * GD)
    mix_grad, mixed4 = lax.optimization_barrier((mix_grad, mixed4))
    mix_grad = lax.all_to_all(mix_grad, everyone, 0, 0, tiled=True)
    back_normed4 = dot_nt(mixed4, w_mix)
    _, shift_back = jax.vjp(
        lambda gain, shift: layer_norm(hidden4, gain, shift), vector[0], vector[1]
    )
    gain_one, shift_one = shift_back(back_normed4)
    pieces = lax.all_to_all(
        back_normed4.astype(BF).reshape(NX, ROWS, D), "x", 0, 0, tiled=True
    )

    def column_sum(value):
        return jnp.sum(value.astype(F32), axis=0)

    def at_group(value):
        return lax.dynamic_update_slice_in_dim(jnp.zeros((D,), F32), value, xi * GD, 0)

    vector_grad = jnp.concatenate(
        [
            jnp.stack(
                [
                    gain_one,
                    shift_one,
                    at_group(column_sum(back_q4)),
                    at_group(column_sum(back_kv4[:, GD:])),
                    column_sum(branch_low),
                    gain_two,
                    shift_two,
                    column_sum(down_low),
                ]
            ),
            column_sum(up_low).reshape(4, D),
        ]
    )
    vector_near = copy_gather(vector_grad, ("c", "y"))
    mix_grad, pieces, vector_near = lax.optimization_barrier((mix_grad, pieces, vector_near))
    vector_total = jnp.sum(
        copy_gather(jnp.sum(vector_near, axis=0), ("x", "z")), axis=0
    )[None]

    back_normed = jnp.sum(pieces.astype(F32), axis=0)
    _, first_back = jax.vjp(lambda h: layer_norm(h, vector[0], vector[1]), hidden)
    input_grad = gradient + first_back(back_normed)[0]

    mix_grad = jnp.sum(mix_grad.reshape(NX, 32, 8, 3 * GD)[:, :, :6].astype(F32), axis=1)
    mix_grad = (
        mix_grad.reshape(NX, 6, 3, GD).transpose(1, 2, 0, 3).reshape(1, 6, 3 * D)
    )
    half = FF // 2
    wide_sum = jnp.sum(
        rest_grad.reshape(NX * NZ, NC, NY, 8, rest_grad.shape[2]).astype(F32), axis=(0, 2)
    )
    top, fill = wide_sum[:, :6], wide_sum[:, 6:, : 3 * D].reshape(NC, 6, D)

    def joined(*parts):
        return jnp.concatenate([part[j] for j in range(NC) for part in parts], axis=1)[None]

    out_grad = joined(top[:, :, 3 * D :])
    fc1_grad = joined(top[:, :, : 2 * D])
    fc2_grad = joined(top[:, :, 2 * D : 3 * D], fill)

    qkv_new = adamw(qkv_weight, qkv_moment, qkv_second, mix_grad, RATE_MATRIX, DECAY_MATRIX)
    out_new = adamw(
        out_weight, out_moment, out_second, out_grad, RATE_MATRIX, DECAY_MATRIX
    )
    fc1_new = adamw(
        fc1_weight, fc1_moment, fc1_second, fc1_grad, RATE_MATRIX, DECAY_MATRIX
    )
    fc2_new = adamw(
        fc2_weight, fc2_moment, fc2_second, fc2_grad, RATE_MATRIX, DECAY_MATRIX
    )
    vec_new = adamw(vectors, vector_moment, vector_second, vector_total, RATE_VECTOR, 0.0)
    return (
        block_out[None],
        input_grad[None],
        *qkv_new,
        *out_new,
        *fc1_new,
        *fc2_new,
        *vec_new,
    )


def solution(mesh):
    grid = Mesh(mesh.devices.reshape(NX, NZ, NC, NY), ("x", "z", "c", "y"))
    rows = P("y", ("x", "z", "c"), None)
    weight = P(None, ("x", "z", "c", "y"), None)
    in_specs = (rows, rows, P()) + (weight,) * 4 + (P(),) + (weight,) * 8 + (P(), P())
    out_specs = (rows, rows) + (weight,) * 12 + (P(), P(), P())
    return jax.shard_map(local, mesh=grid, in_specs=in_specs, out_specs=out_specs, check_vma=False)
```

time: 1610 us -> 393 us (0.24)
  blocking collectives: 541 us -> 0 us
  local copies, waits for them, and re-layouts: 284 us -> 62 us
  matrix products: 236 us -> 40.7 us
  waiting for transfers between devices: 295 us -> 110 us
  starting transfers between devices: 159 us -> 78.6 us
  Pallas kernels: 0 us -> 68.9 us
  other arithmetic: 57.7 us -> 13.1 us
    unnamed x1 -> x0, blocking collectives: 414 us -> none
    all_gather x8 -> x1, waiting for transfers between devices: 274 us -> 3.4 us  [local(): lax.all_gather(rest, everyone, axis=0, tiled=True)]
    dot_general x84 -> x12, matrix products: 236 us -> 40.7 us  [the longest x4 15.8 us: dot_nt(): lax.dot_general(left, right, (((1,), (1,)), ((), ())), preferred_element_...]
    unnamed x218 -> x171, local copies, waits for them, and re-layouts: 197 us -> 27.8 us
    unnamed x32 -> x0, starting transfers between devices: 159 us -> none
    all_to_all x0 -> x11, waiting for transfers between devices: none -> 92.3 us  [the longest x5 35.2 us: copy_gather(): lax.all_to_all(jnp.broadcast_to(part[None], (count,) + part.shape), axes,...]
    psum x1 -> x0, blocking collectives: 80.2 us -> none  [local(): vector_total = lax.psum(jnp.stack(vector_grads, axis=0), ('ctx', 'wsh'))]
    pallas_call x0 -> x5, Pallas kernels: none -> 68.9 us  [call(): pl.pallas_call(kernel, in_specs=specs, out_specs=[pl.BlockSpec(memory_spa...]
  transfers between devices with their start and end apart: 40 -> 22, of which waited for: 9 -> 15; matrix products, arithmetic and copies ran while one was open for 17% -> 14% of each run, Pallas kernels for 0% -> 17%
where the time goes in v1:
time: 393 us; the launch traced here: 390 us
  waiting for transfers between devices  110 us (28%)
  starting transfers between devices  78.6 us (20%)
  Pallas kernels  68.9 us (18%)
  local copies, waits for them, and re-layouts  62 us (16%)
  matrix products  40.7 us (10%)
  between operations  15.9 us (4%)
  other arithmetic  13.1 us (3%)
    pallas_call x5, Pallas kernels, call(): pl.pallas_call(kernel, in_specs=specs, out_specs=[pl.BlockSpec(memory_spa...  68.9 us
    all_to_all x5, starting transfers between devices, copy_gather(): lax.all_to_all(jnp.broadcast_to(part[None], (count,) + part.shape), axes,...  36 us
    all_to_all x5, waiting for transfers between devices, copy_gather(): lax.all_to_all(jnp.broadcast_to(part[None], (count,) + part.shape), axes,...  35.2 us
    unnamed x171, local copies, waits for them, and re-layouts  27.8 us
    all_to_all x1, waiting for transfers between devices, local(): mix_grad = lax.all_to_all(mix_grad, everyone, 0, 0, tiled=True)  16.1 us
    dot_general x4, matrix products, dot_nt(): lax.dot_general(left, right, (((1,), (1,)), ((), ())), preferred_element_...  15.8 us
    all_to_all x1, waiting for transfers between devices, local(): rest_grad = lax.all_to_all(rest_grad, everyone, 0, 0, tiled=True)  13.3 us
    all_to_all x1, waiting for transfers between devices, local(): lax.all_to_all(back_normed4.astype(BF).reshape(NX, ROWS, D), 'x', 0, 0, t...  11.9 us
  transfers between devices with their start and end apart: 22, of which 15 were waited for; matrix products, arithmetic and copies ran while one was open for 14% of the time, Pallas kernels for 17%

profile of v1, /device:TPU:1, one launch (start us, length us, event | category | flops | bytes accessed | tf_op | source)
XLA Modules:
  0.0 389.6 jit_solution(5460770497148719592)
XLA Ops:
  12.5 5.7 %all-to-all-start = ((bf16[16,6,576]{2,1,0:T(8,128)(2,1)}), bf16[16,6,576]{2,1,0:T(8,128)(2,1)S(1)}, u32[]{:S(2)}, u32[]{:S(2)}) async-start(bf16[16,6,576]{2,1,0:T(8,128)(2,1)} %bitcast.27), calls=%async_computation | async-start | bytes 327680 | tf_op jit(solution)/shard_map/all_to_all | solution.py:473
  21.6 3.4 all-to-all-done
  26.1 8.0 %all-to-all-start.1 = ((bf16[8,96,576]{2,1,0:T(8,128)(2,1)}), bf16[8,96,576]{2,1,0:T(8,128)(2,1)S(1)}, u32[]{:S(2)}, u32[]{:S(2)}) async-start(bf16[8,96,576]{2,1,0:T(8,128)(2,1)} %broadcast_in_dim.144), calls=%async_computation.1 | async-start | bytes 1966080 | tf_op jit(solution)/shard_map/all_to_all | solution.py:94
  40.6 7.9 %all-to-all-done.1 = bf16[8,96,576]{2,1,0:T(8,128)(2,1)S(1)} async-done(((bf16[8,96,576]{2,1,0:T(8,128)(2,1)}), bf16[8,96,576]{2,1,0:T(8,128)(2,1)S(1)}, u32[]{:S(2)}, u32[]{:S(2)}) %all-to-all-start.1) | async-done | bytes 884768 | tf_op jit(solution)/shard_map/all_to_all | solution.py:94
  60.6 9.1 %collective-permute-done.4 = bf16[512,384]{1,0:T(8,128)(2,1)S(1)} collective-permute-done((bf16[512,384]{1,0:T(8,128)(2,1)S(1)}, bf16[512,384]{1,0:T(8,128)(2,1)S(1)}, u32[]{:S(2)}, u32[]{:S(2)}) %collective-permute-start.4) | collective-permute-done | bytes 393248 | tf_op jit(solution)/shard_map/ppermute | solution.py:72
  86.1 5.3 %all-to-all-start.2 = ((bf16[8,512,192]{1,2,0:T(8,128)(2,1)}), bf16[8,512,192]{1,2,0:T(8,128)(2,1)}, u32[]{:S(2)}, u32[]{:S(2)}) async-start(bf16[8,512,192]{1,2,0:T(8,128)(2,1)} %broadcast_in_dim.151), calls=%async_computation.2 | async-start | bytes 3145728 | tf_op jit(solution)/shard_map/all_to_all | solution.py:94
  93.4 20.0 %shard_map.341 = (bf16[512,192]{1,0:T(8,128)(2,1)S(1)}, f32[512,192]{1,0:T(8,128)S(1)}, f32[512,128]{1,0:T(8,128)S(1)}) custom-call(s32[144]{0:T(256)S(1)} %pad_add_fusion.2.tab, bf16[512,192]{1,0:T(8,128)(2,1)S(1)} %add_convert_fusion.1.q, bf16[2048,384]{1,0:T(8,128)(2,1)S(1)} %constant_dynamic-update-slice_fusion.5.kv_own, ...), custom_call_target="tpu_custom_call" | custom-call | flops 100000000 | bytes 8388608 | tf_op jit(solution)/shard_map/pallas_call | solution.py:343
  123.5 6.8 %all-to-all-done.3 = bf16[4,128,192]{1,2,0:T(8,128)(2,1)S(1)} async-done(((bf16[4,128,192]{1,2,0:T(8,128)(2,1)}), bf16[4,128,192]{1,2,0:T(8,128)(2,1)S(1)}, u32[]{:S(2)}, u32[]{:S(2)}) %all-to-all-start.3) | async-done | bytes 196640 | tf_op jit(solution)/shard_map/all_to_all | solution.py:499
  130.2 3.4 all-gather.2.cloned.1.call-done
  136.9 6.0 %multiply_convert_fusion = (bf16[128,3072]{1,0:T(8,128)(2,1)}, f32[128,3072]{1,0:T(8,128)}) fusion(f32[3072]{0:T(1024)S(1)} %bitcast.154, bf16[1024,6912]{1,0:T(8,128)(2,1)} %bitcast.149, bf16[128,768]{1,0:T(8,128)(2,1)S(1)} %add_convert_fusion.2, bf16[768,1024]{1,0:T(8,128)(2,1)S(1)} %copy-done.18), kind=kOutput, calls=%fused_computation.34 | convolution fusion | flops 1010696192 | bytes 10432512 | tf_op jit(solution)/shard_map/dot_general | solution.py:517
  142.9 6.3 %convert_reduce_fusion.4 = (f32[3072]{0:T(1024)S(1)}, bf16[128,3072]{1,0:T(8,128)(2,1)S(1)}) fusion(f32[128,3072]{1,0:T(8,128)} %get-tuple-element.260, bf16[1024,6912]{1,0:T(8,128)(2,1)} %bitcast.150, bf16[768,1024]{1,0:T(8,128)(2,1)S(1)} %copy-done.18, bf16[1,128,768]{2,1,0:T(8,128)(2,1)S(1)} %copy-done.28), kind=kOutput, calls=%fused_computation.33 | convolution fusion | flops 1015411712 | bytes 10432512 | tf_op jit(solution)/shard_map/dot_general | solution.py:516
  150.1 5.0 %fusion.4 = f32[128,1024]{1,0:T(8,128)S(1)} fusion(bf16[128,3072]{1,0:T(8,128)(2,1)S(1)} %get-tuple-element.61, bf16[1024,6912]{1,0:T(8,128)(2,1)} %bitcast.151), kind=kOutput, calls=%fused_computation.7 | convolution fusion | flops 805306368 | bytes 7602176 | tf_op jit(solution)/shard_map/dot_general | solution.py:113
  161.4 3.5 all-to-all-start.4
  164.9 5.5 %all-to-all-done.4 = bf16[4,128,192]{1,2,0:T(8,128)(2,1)S(1)} async-done(((bf16[4,128,192]{1,2,0:T(8,128)(2,1)}), bf16[4,128,192]{1,2,0:T(8,128)(2,1)S(1)}, u32[]{:S(2)}, u32[]{:S(2)}) %all-to-all-start.4) | async-done | bytes 196640 | tf_op jit(solution)/shard_map/all_to_all | solution.py:530
  181.2 15.4 %all-to-all-start.5 = ((bf16[8,512,256]{2,1,0:T(8,128)(2,1)}), bf16[8,512,256]{2,1,0:T(8,128)(2,1)S(1)}, u32[]{:S(2)}, u32[]{:S(2)}) async-start(bf16[8,512,256]{2,1,0:T(8,128)(2,1)} %broadcast_in_dim.155), calls=%async_computation.5 | async-start | bytes 4194304 | tf_op jit(solution)/shard_map/all_to_all | solution.py:94
  204.0 7.9 %shard_map.343 = bf16[1024,2688]{1,0:T(8,128)(2,1)} custom-call(bf16[256,768]{1,0:T(8,128)(2,1)S(1)} %pad_maximum_fusion.4.att, bf16[256,768]{1,0:T(8,128)(2,1)S(1)} %pad_maximum_fusion.5.two, bf16[256,768]{1,0:T(8,128)(2,1)S(1)} %pad_maximum_fusion.6.down, bf16[256,384]{1,0:T(8,128)(2,1)S(1)} %pad_maximum_fusion.7.branch, ...), custom_call_target="tpu_custom_call" | custom-call | flops 100000000 | bytes 8388608 | tf_op jit(solution)/shard_map/pallas_call | solution.py:343
  211.9 10.8 %all-to-all-done.5 = bf16[8,512,256]{2,1,0:T(8,128)(2,1)S(1)} async-done(((bf16[8,512,256]{2,1,0:T(8,128)(2,1)}), bf16[8,512,256]{2,1,0:T(8,128)(2,1)S(1)}, u32[]{:S(2)}, u32[]{:S(2)}) %all-to-all-start.5) | async-done | bytes 2097184 | tf_op jit(solution)/shard_map/all_to_all | solution.py:94
  224.0 5.4 %all-to-all-start.6 = ((bf16[128,8,2688]{2,1,0:T(8,128)(2,1)}), bf16[128,8,2688]{2,1,0:T(8,128)(2,1)}, u32[]{:S(2)}, u32[]{:S(2)}) async-start(bf16[128,8,2688]{2,1,0:T(8,128)(2,1)} %bitcast.136), calls=%async_computation.6 | async-start | bytes 11010048 | tf_op jit(solution)/shard_map/all_to_all | solution.py:560
  229.6 3.7 convolution_convert_fusion.1
  236.2 5.4 %fusion.2 = f32[128,1024]{1,0:T(8,128)S(1)} fusion(bf16[128,3072]{1,0:T(8,128)(2,1)} %get-tuple-element.62, bf16[1024,6912]{1,0:T(8,128)(2,1)} %bitcast.153), kind=kOutput, calls=%fused_computation.5 | convolution fusion | flops 805306368 | bytes 7602176 | tf_op jit(solution)/shard_map/dot_general | solution.py:113
  244.0 15.7 %shard_map.344 = bf16[512,192]{1,0:T(8,128)(2,1)S(1)} custom-call(s32[144]{0:T(256)S(1)} %pad_add_fusion.2.tab, bf16[512,192]{1,0:T(8,128)(2,1)S(1)} %add_convert_fusion.1.q, bf16[512,192]{1,0:T(8,128)(2,1)S(1)} %bitcast.134, f32[512,128]{1,0:T(8,128)S(1)} %copy-done.13, bf16[2048,384]{1,0:T(8,128)(2,1)S(1)} %copy-done.3, bf16[2048,384]{1,0:T(8,128)(2,1)S(1)} %copy-done.5), custom_call_target="tpu_custom_call" | custom-call | flops 100000000 | bytes 8388608 | tf_op jit(solution)/shard_map/pallas_call | solution.py:343
  261.6 24.2 %shard_map.345 = bf16[512,384]{1,0:T(8,128)(2,1)S(1)} custom-call(s32[144]{0:T(256)S(1)} %pad_add_fusion.2.tab, bf16[512,384]{1,0:T(8,128)(2,1)S(1)} %copy-done.9, bf16[4096,192]{1,0:T(8,128)(2,1)S(1)} %bitcast.131, bf16[4096,256]{1,0:T(8,128)(2,1)S(1)} %bitcast.132, bf16[8,128]{1,0:T(8,128)(2,1)S(1)} %copy-done.17), custom_call_target="tpu_custom_call" | custom-call | flops 100000000 | bytes 8388608 | tf_op jit(solution)/shard_map/pallas_call | solution.py:343
  285.8 13.3 %all-to-all-done.6 = bf16[128,8,2688]{2,1,0:T(8,128)(2,1)} async-done(((bf16[128,8,2688]{2,1,0:T(8,128)(2,1)}), bf16[128,8,2688]{2,1,0:T(8,128)(2,1)}, u32[]{:S(2)}, u32[]{:S(2)}) %all-to-all-start.6) | async-done | bytes 5505056 | tf_op jit(solution)/shard_map/all_to_all | solution.py:560
  307.0 3.6 all-to-all-start.9
  310.7 3.4 convert_reduce_fusion
  314.2 3.9 %all-to-all-done.9 = f32[8,12,768]{2,1,0:T(8,128)S(1)} async-done(((f32[8,12,768]{2,1,0:T(8,128)}), f32[8,12,768]{2,1,0:T(8,128)S(1)}, u32[]{:S(2)}, u32[]{:S(2)}) %all-to-all-start.9) | async-done | bytes 294944 | tf_op jit(solution)/shard_map/all_to_all | solution.py:94
  318.2 3.5 all-to-all-start.8
  321.8 11.9 %all-to-all-done.8 = bf16[4,128,768]{2,1,0:T(8,128)(2,1)S(1)} async-done(((bf16[4,128,768]{2,1,0:T(8,128)(2,1)}), bf16[4,128,768]{2,1,0:T(8,128)(2,1)S(1)}, u32[]{:S(2)}, u32[]{:S(2)}) %all-to-all-start.8) | async-done | bytes 786464 | tf_op jit(solution)/shard_map/all_to_all | solution.py:576
  333.7 5.0 %all-to-all-start.7 = ((bf16[128,8,576]{2,1,0:T(8,128)(2,1)}), bf16[128,8,576]{2,1,0:T(8,128)(2,1)S(1)}, u32[]{:S(2)}, u32[]{:S(2)}) async-start(bf16[128,8,576]{2,1,0:T(8,128)(2,1)} %bitcast.49), calls=%async_computation.7 | async-start | bytes 2621440 | tf_op jit(solution)/shard_map/all_to_all | solution.py:570
  345.1 16.1 %all-to-all-done.7 = bf16[128,8,576]{2,1,0:T(8,128)(2,1)S(1)} async-done(((bf16[128,8,576]{2,1,0:T(8,128)(2,1)}), bf16[128,8,576]{2,1,0:T(8,128)(2,1)S(1)}, u32[]{:S(2)}, u32[]{:S(2)}) %all-to-all-start.7) | async-done | bytes 1179680 | tf_op jit(solution)/shard_map/all_to_all | solution.py:570
  363.0 3.7 all-to-all-start.10
  370.4 10.0 %all-to-all-done.10 = f32[16,12,768]{2,1,0:T(8,128)S(1)} async-done(((f32[16,12,768]{2,1,0:T(8,128)}), f32[16,12,768]{2,1,0:T(8,128)S(1)}, u32[]{:S(2)}, u32[]{:S(2)}) %all-to-all-start.10) | async-done | bytes 589856 | tf_op jit(solution)/shard_map/all_to_all | solution.py:94
  (335 shorter events, 115.0 us)
Async XLA Ops:
  7.2 26.9 %collective-permute-start = (bf16[128,768]{1,0:T(8,128)(2,1)}, bf16[128,768]{1,0:T(8,128)(2,1)S(1)}, u32[]{:S(2)}, u32[]{:S(2)}) collective-permute-start(bf16[128,768]{1,0:T(8,128)(2,1)} %bitcast.137), channel_id=1, source_target_pairs={{0,32},{32,64},{64,96},{96,0},{1,33},{33,65},{65,97},{97,1},{2,34}... | collective-permute-start | bytes 589832 | tf_op jit(solution)/shard_map/ppermute | solution.py:72
  9.3 25.1 %collective-permute-start.1 = (bf16[128,768]{1,0:T(8,128)(2,1)}, bf16[128,768]{1,0:T(8,128)(2,1)S(1)}, u32[]{:S(2)}, u32[]{:S(2)}) collective-permute-start(bf16[128,768]{1,0:T(8,128)(2,1)} %bitcast.138), channel_id=1, source_target_pairs={{0,96},{32,0},{64,32},{96,64},{1,97},{33,1},{65,33},{97,65},{2,98}... | collective-permute-start | bytes 589832 | tf_op jit(solution)/shard_map/ppermute | solution.py:73
  12.5 12.5 %all-to-all-start = ((bf16[16,6,576]{2,1,0:T(8,128)(2,1)}), bf16[16,6,576]{2,1,0:T(8,128)(2,1)S(1)}, u32[]{:S(2)}, u32[]{:S(2)}) async-start(bf16[16,6,576]{2,1,0:T(8,128)(2,1)} %bitcast.27), calls=%async_computation | async-start | bytes 327680 | tf_op jit(solution)/shard_map/all_to_all | solution.py:473
  26.1 22.4 %all-to-all-start.1 = ((bf16[8,96,576]{2,1,0:T(8,128)(2,1)}), bf16[8,96,576]{2,1,0:T(8,128)(2,1)S(1)}, u32[]{:S(2)}, u32[]{:S(2)}) async-start(bf16[8,96,576]{2,1,0:T(8,128)(2,1)} %broadcast_in_dim.144), calls=%async_computation.1 | async-start | bytes 1966080 | tf_op jit(solution)/shard_map/all_to_all | solution.py:94
  34.1 99.5 %all-gather.2.cloned.1.call-start = ((), (), s32[]{:S(2)}) async-start(), calls=%async_computation.11 | async-start | bytes 14266368 | tf_op jit(solution)/shard_map/all_gather | solution.py:481
  34.1 5.7 %collective-permute-start.2 = (bf16[64,768]{1,0:T(8,128)(2,1)S(1)}, bf16[64,768]{1,0:T(8,128)(2,1)S(1)}, u32[]{:S(2)}, u32[]{:S(2)}) collective-permute-start(bf16[64,768]{1,0:T(8,128)(2,1)S(1)} %slice.192), channel_id=1, source_target_pairs={{0,32},{32,64},{64,96},{96,0},{1,33},{33,65},{65,97},{97,1},{2,34}... | collective-permute-start | bytes 294920 | tf_op jit(solution)/shard_map/ppermute | solution.py:74
  34.4 5.4 %collective-permute-start.3 = (bf16[64,768]{1,0:T(8,128)(2,1)S(1)}, bf16[64,768]{1,0:T(8,128)(2,1)S(1)}, u32[]{:S(2)}, u32[]{:S(2)}) collective-permute-start(bf16[64,768]{1,0:T(8,128)(2,1)S(1)} %slice.193), channel_id=1, source_target_pairs={{0,96},{32,0},{64,32},{96,64},{1,97},{33,1},{65,33},{97,65},{2,98}... | collective-permute-start | bytes 294920 | tf_op jit(solution)/shard_map/ppermute | solution.py:75
  57.9 17.8 %copy-start.8 = (bf16[512,384]{1,0:T(8,128)(2,1)}, bf16[512,384]{1,0:T(8,128)(2,1)S(1)}, u32[]{:S(2)}) copy-start(bf16[512,384]{1,0:T(8,128)(2,1)S(1)} %get-tuple-element.226.kv) | copy-start | bytes 1179652
  57.9 20.8 %copy-start.69 = (s32[32]{0:T(128)S(1)}, s32[32]{0:T(128)}, u32[]{:S(2)}) copy-start(s32[32]{0:T(128)} %param.26) | copy-start | bytes 388
  57.9 11.8 %collective-permute-start.4 = (bf16[512,384]{1,0:T(8,128)(2,1)S(1)}, bf16[512,384]{1,0:T(8,128)(2,1)S(1)}, u32[]{:S(2)}, u32[]{:S(2)}) collective-permute-start(bf16[512,384]{1,0:T(8,128)(2,1)S(1)} %get-tuple-element.226.kv), channel_id=1, source_target_pairs={{0,8},{8,16},{16,24},{24,0},{1,9},{9,17},{17,25},{25,1},{2,10},{10... | collective-permute-start | bytes 1179656 | tf_op jit(solution)/shard_map/ppermute | solution.py:72
  58.2 11.6 %collective-permute-start.5 = (bf16[512,384]{1,0:T(8,128)(2,1)S(1)}, bf16[512,384]{1,0:T(8,128)(2,1)S(1)}, u32[]{:S(2)}, u32[]{:S(2)}) collective-permute-start(bf16[512,384]{1,0:T(8,128)(2,1)S(1)} %get-tuple-element.226.kv), channel_id=1, source_target_pairs={{0,24},{8,0},{16,8},{24,16},{1,25},{9,1},{17,9},{25,17},{2,26},{10... | collective-permute-start | bytes 1179656 | tf_op jit(solution)/shard_map/ppermute | solution.py:73
  69.7 5.8 %collective-permute-start.6 = (bf16[256,384]{1,0:T(8,128)(2,1)S(1)}, bf16[256,384]{1,0:T(8,128)(2,1)S(1)}, u32[]{:S(2)}, u32[]{:S(2)}) collective-permute-start(bf16[256,384]{1,0:T(8,128)(2,1)S(1)} %slice.197), channel_id=1, source_target_pairs={{0,8},{8,16},{16,24},{24,0},{1,9},{9,17},{17,25},{25,1},{2,10},{10... | collective-permute-start | bytes 589832 | tf_op jit(solution)/shard_map/ppermute | solution.py:74
  69.9 5.8 %collective-permute-start.7 = (bf16[256,384]{1,0:T(8,128)(2,1)S(1)}, bf16[256,384]{1,0:T(8,128)(2,1)S(1)}, u32[]{:S(2)}, u32[]{:S(2)}) collective-permute-start(bf16[256,384]{1,0:T(8,128)(2,1)S(1)} %slice.198), channel_id=1, source_target_pairs={{0,24},{8,0},{16,8},{24,16},{1,25},{9,1},{17,9},{25,17},{2,26},{10... | collective-permute-start | bytes 589832 | tf_op jit(solution)/shard_map/ppermute | solution.py:75
  75.7 7.2 %collective-permute-start.8 = (bf16[2048,384]{1,0:T(8,128)(2,1)S(1)}, bf16[2048,384]{1,0:T(8,128)(2,1)S(1)}, u32[]{:S(2)}, u32[]{:S(2)}) collective-permute-start(bf16[2048,384]{1,0:T(8,128)(2,1)S(1)} %constant_dynamic-update-slice_fusion.5.kv_own), channel_id=1, source_target_pairs={{0,4},{4,0},{1,5},{5,1},{2,6},{6,2},{3,7},{7,3},{8,12},{12,8},{9,1... | collective-permute-start | bytes 4718600 | tf_op jit(solution)/shard_map/ppermute | solution.py:89
  86.1 32.2 %all-to-all-start.2 = ((bf16[8,512,192]{1,2,0:T(8,128)(2,1)}), bf16[8,512,192]{1,2,0:T(8,128)(2,1)}, u32[]{:S(2)}, u32[]{:S(2)}) async-start(bf16[8,512,192]{1,2,0:T(8,128)(2,1)} %broadcast_in_dim.151), calls=%async_computation.2 | async-start | bytes 3145728 | tf_op jit(solution)/shard_map/all_to_all | solution.py:94
  93.4 40.2 %copy-start.61 = (f32[768]{0:T(1024)S(1)}, f32[768]{0:T(1024)}, u32[]{:S(2)}) copy-start(f32[768]{0:T(1024)} %get-tuple-element.201) | copy-start | bytes 9220
  120.1 10.1 %all-to-all-start.3 = ((bf16[4,128,192]{1,2,0:T(8,128)(2,1)}), bf16[4,128,192]{1,2,0:T(8,128)(2,1)S(1)}, u32[]{:S(2)}, u32[]{:S(2)}) async-start(bf16[4,128,192]{1,2,0:T(8,128)(2,1)} %copy.333), calls=%async_computation.3 | async-start | bytes 393216 | tf_op jit(solution)/shard_map/all_to_all | solution.py:499
  136.5 20.4 %copy-start.20 = (f32[128,768]{1,0:T(8,128)}, f32[128,768]{1,0:T(8,128)S(1)}, u32[]{:S(2)}) copy-start(f32[128,768]{1,0:T(8,128)S(1)} %get-tuple-element.257) | copy-start | bytes 1179652
  161.4 9.0 %all-to-all-start.4 = ((bf16[4,128,192]{1,2,0:T(8,128)(2,1)}), bf16[4,128,192]{1,2,0:T(8,128)(2,1)S(1)}, u32[]{:S(2)}, u32[]{:S(2)}) async-start(bf16[4,128,192]{1,2,0:T(8,128)(2,1)} %bitcast.43), calls=%async_computation.4 | async-start | bytes 393216 | tf_op jit(solution)/shard_map/all_to_all | solution.py:530
  178.4 18.2 %collective-permute-start.9 = (bf16[128,5760]{1,0:T(8,128)(2,1)}, bf16[128,5760]{1,0:T(8,128)(2,1)}, u32[]{:S(2)}, u32[]{:S(2)}) collective-permute-start(bf16[128,5760]{1,0:T(8,128)(2,1)} %get-tuple-element.236), channel_id=1, source_target_pairs={{0,4},{4,0},{1,5},{5,1},{2,6},{6,2},{3,7},{7,3},{8,12},{12,8},{9,1... | collective-permute-start | bytes 4423688 | tf_op jit(solution)/shard_map/ppermute | solution.py:549
  181.2 41.4 %all-to-all-start.5 = ((bf16[8,512,256]{2,1,0:T(8,128)(2,1)}), bf16[8,512,256]{2,1,0:T(8,128)(2,1)S(1)}, u32[]{:S(2)}, u32[]{:S(2)}) async-start(bf16[8,512,256]{2,1,0:T(8,128)(2,1)} %broadcast_in_dim.155), calls=%async_computation.5 | async-start | bytes 4194304 | tf_op jit(solution)/shard_map/all_to_all | solution.py:94
  211.9 17.7 %copy-start.64 = (f32[512]{0:T(512)S(1)}, f32[512]{0:T(512)}, u32[]{:S(2)}) copy-start(f32[512]{0:T(512)} %copy-done.63) | copy-start | bytes 6148
  211.9 17.7 %copy-start.66 = (f32[768]{0:T(1024)S(1)}, f32[768]{0:T(1024)}, u32[]{:S(2)}) copy-start(f32[768]{0:T(1024)} %copy-done.65) | copy-start | bytes 9220
  211.9 17.7 %copy-start.68 = (f32[512]{0:T(512)S(1)}, f32[512]{0:T(512)}, u32[]{:S(2)}) copy-start(f32[512]{0:T(512)} %copy-done.67) | copy-start | bytes 6148
  224.0 75.0 %all-to-all-start.6 = ((bf16[128,8,2688]{2,1,0:T(8,128)(2,1)}), bf16[128,8,2688]{2,1,0:T(8,128)(2,1)}, u32[]{:S(2)}, u32[]{:S(2)}) async-start(bf16[128,8,2688]{2,1,0:T(8,128)(2,1)} %bitcast.136), calls=%async_computation.6 | async-start | bytes 11010048 | tf_op jit(solution)/shard_map/all_to_all | solution.py:560
  307.0 11.1 %all-to-all-start.9 = ((f32[8,12,768]{2,1,0:T(8,128)}), f32[8,12,768]{2,1,0:T(8,128)S(1)}, u32[]{:S(2)}, u32[]{:S(2)}) async-start(f32[8,12,768]{2,1,0:T(8,128)} %broadcast_in_dim.156), calls=%async_computation.9 | async-start | bytes 786432 | tf_op jit(solution)/shard_map/all_to_all | solution.py:94
  318.2 15.5 %all-to-all-start.8 = ((bf16[4,128,768]{2,1,0:T(8,128)(2,1)}), bf16[4,128,768]{2,1,0:T(8,128)(2,1)S(1)}, u32[]{:S(2)}, u32[]{:S(2)}) async-start(bf16[4,128,768]{2,1,0:T(8,128)(2,1)} %bitcast.50), calls=%async_computation.8 | async-start | bytes 1572864 | tf_op jit(solution)/shard_map/all_to_all | solution.py:576
  321.7 21.1 %copy-start.45 = (f32[1,6,3072]{2,0,1:T(1,128)S(1)}, f32[1,6,3072]{2,0,1:T(1,128)}, u32[]{:S(2)}) copy-start(f32[1,6,3072]{2,0,1:T(1,128)} %param.30) | copy-start | bytes 221188
  321.8 21.1 %copy-start.51 = (f32[1,6,3072]{2,0,1:T(1,128)S(1)}, f32[1,6,3072]{2,0,1:T(1,128)}, u32[]{:S(2)}) copy-start(f32[1,6,3072]{2,0,1:T(1,128)} %param.39) | copy-start | bytes 221188
  321.8 21.1 %copy-start.52 = (f32[1,6,3072]{2,0,1:T(1,128)S(1)}, f32[1,6,3072]{2,0,1:T(1,128)}, u32[]{:S(2)}) copy-start(f32[1,6,3072]{2,0,1:T(1,128)} %param.38) | copy-start | bytes 221188
  333.7 27.6 %all-to-all-start.7 = ((bf16[128,8,576]{2,1,0:T(8,128)(2,1)}), bf16[128,8,576]{2,1,0:T(8,128)(2,1)S(1)}, u32[]{:S(2)}, u32[]{:S(2)}) async-start(bf16[128,8,576]{2,1,0:T(8,128)(2,1)} %bitcast.49), calls=%async_computation.7 | async-start | bytes 2621440 | tf_op jit(solution)/shard_map/all_to_all | solution.py:570
  363.0 17.4 %all-to-all-start.10 = ((f32[16,12,768]{2,1,0:T(8,128)}), f32[16,12,768]{2,1,0:T(8,128)S(1)}, u32[]{:S(2)}, u32[]{:S(2)}) async-start(f32[16,12,768]{2,1,0:T(8,128)} %broadcast_in_dim.160), calls=%async_computation.10 | async-start | bytes 1572864 | tf_op jit(solution)/shard_map/all_to_all | solution.py:94
  (63 other events, 400.4 us)
Sparse Core Ops, SparseCore 0:
  52.3 81.2 all-gather.1
